TPU v7x, 32 devices: a whole 2x2x4 slice. The times are simulated.
32 devices in a mesh: parts: 2 (over y), dp: 4 (over x, core), tensor: 4 (over z).
Axes of the slice: x: 2, y: 2, z: 4, core: 2. Of those that a mesh axis runs over, the one named last changes fastest.
Arguments:
- tokens: bfloat16 [16384, 8192], P(('parts', 'dp'), 'tensor'), parts along dimension 0, may hold values from -6 to 6
- target: bfloat16 [16384, 1024], P(('parts', 'dp'), 'tensor'), parts along dimension 0, may hold values from -6 to 6
- task_embed: bfloat16 [64, 2048], P('parts'), parts along dimension 0, may hold values from -6 to 6
- head_a: bfloat16 [2048, 16, 8192], P(None, 'dp', 'tensor'), may hold values from -0.0014648438 to 0.0014648438
- head_b: bfloat16 [2048, 16, 1024], P(None, 'dp', 'tensor'), may hold values from -0.00390625 to 0.00390625
- base_v: bfloat16 [8192, 1024], P('tensor', 'dp'), may hold values from -0.0625 to 0.0625
- block_tenant: int32 [128], P('parts'), parts along dimension 0, may hold values from 0 to 31, as said below
- block_count: int32 [64], P('parts'), parts along dimension 0, may hold values from 1 to 16, as said below
Outputs:
- grad_head_a: bfloat16 [4096, 16, 8192], P('parts', 'dp', 'tensor'), parts along dimension 0
- grad_head_b: bfloat16 [4096, 16, 1024], P('parts', 'dp', 'tensor'), parts along dimension 0
There are 2 independent parts, one for each index of `parts`. A program takes and returns all parts, laid end to end along the dimension named above; an argument that names none is the same for every part. Nothing has to cross between parts.
Inputs may be any that keep to these rules, and one draw needn't show every extreme that they name: `block_tenant`: entries i * 16 to (i + 1) * 16 - 1 are the blocks of group i of dp. All blocks of a tenant lie in one group, and every tenant has a block. A group holds 1 to 15 tenants; some group holds exactly 15 and some exactly 1; groups 2i and 2i + 1 hold 16 tenants together. block_count[t] is the number of entries of block_tenant equal to t.
All inputs are finite; a program needn't handle non-finite values.
Results may differ from a plain program's by a relative error of at most 0.018.
Values may be sent and summed in bfloat16 or wider, within the bound.
A program may use at most 256 MiB of HBM per device.

v0:
```python
import jax
import jax.numpy as jnp
from jax import lax
from jax.sharding import PartitionSpec as P

R = 16
BLOCK = 128
TCAP = 15


def owner_tables(block_tenant, tenants, blocks, groups):
    ids = jnp.arange(tenants, dtype=jnp.int32)
    block_group = jnp.arange(blocks * groups, dtype=jnp.int32) // blocks
    member = block_tenant[None, :] == ids[:, None]
    owner = jnp.max(jnp.where(member, block_group[None, :], -1), axis=1)
    earlier = (owner[None, :] == owner[:, None]) & (ids[None, :] < ids[:, None])
    slot = jnp.sum(earlier.astype(jnp.int32), axis=1)
    group_ids = jnp.arange(groups, dtype=jnp.int32)
    slot_ids = jnp.arange(TCAP, dtype=jnp.int32)
    place = (owner[None, None, :] == group_ids[:, None, None]) & (
        slot[None, None, :] == slot_ids[None, :, None]
    )
    holder = jnp.sum(jnp.where(place, ids[None, None, :], 0), axis=2)
    return (owner, slot, holder)


def body(tokens, target, task_embed, head_a, head_b, base_v, block_tenant, block_count):
    groups = lax.axis_size("dp")
    group_now = lax.axis_index("dp")
    tenants, hidden = task_embed.shape
    rank_part = head_a.shape[1]
    width_part = head_a.shape[2]
    kv_part = head_b.shape[2]
    rows = tokens.shape[0]
    blocks = rows // BLOCK
    owner, slot, holder = owner_tables(block_tenant, tenants, blocks, groups)
    flat_a = jnp.dot(
        task_embed,
        head_a.reshape(hidden, rank_part * width_part),
        preferred_element_type=jnp.float32,
    )
    flat_a = flat_a.astype(jnp.bfloat16).reshape(tenants, rank_part, width_part)
    flat_b = jnp.dot(
        task_embed, head_b.reshape(hidden, rank_part * kv_part), preferred_element_type=jnp.float32
    )
    flat_b = flat_b.astype(jnp.bfloat16).reshape(tenants, rank_part, kv_part)
    full_a, full_b = (
        lax.all_gather(flat_a, "dp", axis=1, tiled=True),
        lax.all_gather(flat_b, "dp", axis=1, tiled=True),
    )
    mine = holder[group_now]
    own_a = full_a[mine]
    own_b = full_b[mine]
    own_blocks = lax.dynamic_slice_in_dim(block_tenant, group_now * blocks, blocks)
    block_slot = slot[own_blocks]
    pick_slot = (block_slot[:, None] == jnp.arange(TCAP, dtype=jnp.int32)[None, :]).astype(
        jnp.float32
    )
    factor_a = own_a[block_slot]
    factor_b = own_b[block_slot]
    x_blocks = tokens.reshape(blocks, BLOCK, width_part)
    partial_rank = jnp.einsum(
        "brd,bmd->brm", factor_a, x_blocks, preferred_element_type=jnp.float32
    )
    low_rank = lax.psum(partial_rank.astype(jnp.bfloat16), "tensor")
    base_terms = jnp.dot(
        tokens, lax.all_gather(base_v, "dp", axis=1, tiled=True), preferred_element_type=jnp.float32
    )
    base = lax.psum_scatter(
        base_terms.astype(jnp.bfloat16), "tensor", scatter_dimension=1, tiled=True
    ).astype(jnp.float32)
    adapted = jnp.einsum("brm,brc->bmc", low_rank, factor_b, preferred_element_type=jnp.float32)
    projected = base.reshape(blocks, BLOCK, kv_part) + 2.0 * adapted
    weight = 1.0 / (BLOCK * block_count[own_blocks].astype(jnp.float32))
    error = projected - target.reshape(blocks, BLOCK, kv_part).astype(jnp.float32)
    error_grad = (error * weight[:, None, None]).astype(jnp.bfloat16)
    partial_back = jnp.einsum(
        "bmc,brc->brm", error_grad, factor_b, preferred_element_type=jnp.float32
    )
    rank_grad = lax.psum(partial_back.astype(jnp.bfloat16), "tensor")
    block_grad_a = 2.0 * jnp.einsum(
        "brm,bmd->brd", rank_grad, x_blocks, preferred_element_type=jnp.float32
    )
    block_grad_b = 2.0 * jnp.einsum(
        "brm,bmc->brc", low_rank, error_grad, preferred_element_type=jnp.float32
    )
    grad_a = jnp.dot(
        pick_slot.T, block_grad_a.reshape(blocks, R * width_part), precision=lax.Precision.HIGHEST
    )
    grad_b = jnp.dot(
        pick_slot.T, block_grad_b.reshape(blocks, R * kv_part), precision=lax.Precision.HIGHEST
    )
    grad_a = grad_a.astype(jnp.bfloat16)
    grad_b = grad_b.astype(jnp.bfloat16)
    every_a, every_b = (
        lax.all_gather(grad_a.reshape(TCAP, R, width_part), "dp", axis=0, tiled=True),
        lax.all_gather(grad_b.reshape(TCAP, R, kv_part), "dp", axis=0, tiled=True),
    )
    index = owner * TCAP + slot
    tenant_a = lax.dynamic_slice_in_dim(every_a[index], group_now * rank_part, rank_part, 1)
    tenant_b = lax.dynamic_slice_in_dim(every_b[index], group_now * rank_part, rank_part, 1)
    grad_head_a = jnp.einsum(
        "th,tk->hk",
        task_embed,
        tenant_a.reshape(tenants, rank_part * width_part),
        preferred_element_type=jnp.float32,
    )
    grad_head_b = jnp.einsum(
        "th,tk->hk",
        task_embed,
        tenant_b.reshape(tenants, rank_part * kv_part),
        preferred_element_type=jnp.float32,
    )
    grad_head_a = grad_head_a.astype(jnp.bfloat16).reshape(hidden, rank_part, width_part)
    grad_head_b = grad_head_b.astype(jnp.bfloat16).reshape(hidden, rank_part, kv_part)
    return (grad_head_a, grad_head_b)


def solution(mesh):
    return jax.shard_map(
        body,
        mesh=mesh,
        in_specs=(
            P(("parts", "dp"), "tensor"),
            P(("parts", "dp"), "tensor"),
            P("parts", None),
            P(None, "dp", "tensor"),
            P(None, "dp", "tensor"),
            P("tensor", "dp"),
            P("parts"),
            P("parts"),
        ),
        out_specs=(P("parts", "dp", "tensor"), P("parts", "dp", "tensor")),
        check_vma=False,
    )
```

profile of v0, /device:TPU:0, one launch (start us, length us, event | category | flops | bytes accessed | tf_op | source)
XLA Modules:
  0.0 389.1 jit_solution(17578929376776055138)
XLA Ops:
  7.2 30.0 %copy.42 = bf16[256,8,4,2048]{3,1,2,0:T(8,128)(2,1)} copy(bf16[256,8,4,2048]{3,2,1,0:T(4,128)(2,1)} %bitcast.75) | data formatting | bytes 67108864
  37.3 13.6 %convolution_convert_fusion.2 = bf16[32,8192]{1,0:T(8,128)(2,1)S(1)} fusion(bf16[32,2048]{1,0:T(8,128)(2,1)S(1)} %copy-done, bf16[2048,8192]{1,0:T(8,128)(2,1)} %bitcast.72), kind=kOutput, calls=%fused_computation.10 | convolution fusion | flops 1074003968 | bytes 34209792 | tf_op jit(solution)/shard_map/dot_general | solution.py:37
  50.9 0.8 copy.51
  51.8 0.7 all-gather.4.cloned.1.call-update
  53.0 0.7 gather_fusion
  54.3 22.9 %all-gather.6.cloned.1.call-done = bf16[32,16,2048]{2,0,1:T(8,128)(2,1)} async-done(((bf16[32,4,2048]{2,0,1:T(8,128)(2,1)}), bf16[32,16,2048]{2,0,1:T(8,128)(2,1)}) %all-gather.6.cloned.1.call-update) | async-done | bytes 2097168 | tf_op jit(solution)/shard_map/all_gather | solution.py:48
  77.2 2.7 copy.36
  79.9 0.6 gather_fusion.3
  80.6 0.6 gather_fusion.4
  81.2 6.3 %convolution_convert_fusion.7 = bf16[16,16,128]{2,1,0:T(8,128)(2,1)} fusion(bf16[16,16,2048]{2,1,0:T(8,128)(2,1)S(1)} %gather_fusion.4, bf16[16,128,2048]{2,1,0:T(8,128)(2,1)} %bitcast.73), kind=kOutput, calls=%fused_computation.21 | convolution fusion | flops 134250496 | bytes 9502720 | tf_op jit(solution)/shard_map/brd,bmd->brm/dot_general | solution.py:62
  87.6 26.2 %all-gather.4.cloned.1.call-done = bf16[2048,1024]{1,0:T(8,128)(2,1)} async-done(((bf16[2048,256]{1,0:T(8,128)(2,1)}), bf16[2048,1024]{1,0:T(8,128)(2,1)}) %all-gather.4.cloned.1.call-update) | async-done | bytes 4194320 | tf_op jit(solution)/shard_map/all_gather | solution.py:67
  113.8 13.8 %convolution_convert_fusion.4 = bf16[2048,1024]{1,0:T(8,128)(2,1)} fusion(bf16[2048,2048]{1,0:T(8,128)(2,1)} %param.8, bf16[2048,1024]{1,0:T(8,128)(2,1)} %all-gather.4.cloned.1.call-done), kind=kOutput, calls=%fused_computation.12 | convolution fusion | flops 8592031744 | bytes 16777216 | tf_op jit(solution)/shard_map/dot_general | solution.py:66
  127.8 3.2 copy.41
  131.1 0.8 convolution_convert_fusion.8
  131.9 5.8 %all_gather.15 = bf16[32,16,256]{2,0,1:T(8,128)(2,1)S(1)} all-gather(bf16[32,4,256]{2,0,1:T(8,128)(2,1)S(1)} %bitcast.93), channel_id=1, replica_groups=mesh['parts'=2,'dp'=4,'tensor'=4] {'dp'}, dimensions={1}, use_global_device_ids=true | all-gather | bytes 327680 | tf_op jit(solution)/shard_map/all_gather | solution.py:49
  139.0 0.7 gather_fusion.5
  139.7 11.0 %all-reduce.3.cloned.1.call-done = bf16[16,16,128]{2,1,0:T(8,128)(2,1)} async-done(((bf16[16,16,128]{2,1,0:T(8,128)(2,1)}), bf16[16,16,128]{2,1,0:T(8,128)(2,1)}) %all-reduce.3.cloned.1.call-update) | async-done | bytes 65552 | tf_op jit(solution)/shard_map/psum | solution.py:65
  150.7 79.3 %reduce-scatter.2.cloned.1.call-done = bf16[2048,256]{1,0:T(8,128)(2,1)} async-done(((bf16[2048,1024]{1,0:T(8,128)(2,1)}), bf16[2048,256]{1,0:T(8,128)(2,1)}) %reduce-scatter.2.cloned.1.call-update) | async-done | bytes 1048592 | tf_op jit(solution)/shard_map/reduce_scatter | solution.py:69
  230.0 2.0 fusion.1
  232.0 1.0 convolution_convert_fusion.6
  233.1 34.6 %all-reduce.5.cloned.1.call-done = bf16[16,16,128]{2,1,0:T(8,128)(2,1)} async-done(((bf16[16,16,128]{2,1,0:T(8,128)(2,1)}), bf16[16,16,128]{2,1,0:T(8,128)(2,1)}) %all-reduce.5.cloned.1.call-update) | async-done | bytes 65552 | tf_op jit(solution)/shard_map/psum | solution.py:80
  267.7 4.6 %convolution_multiply_fusion = f32[16,16,2048]{2,1,0:T(8,128)S(1)} fusion(bf16[16,16,128]{2,1,0:T(8,128)(2,1)} %all-reduce.5.cloned.1.call-done, bf16[16,128,2048]{2,1,0:T(8,128)(2,1)} %bitcast.74), kind=kOutput, calls=%fused_computation.14 | convolution fusion | flops 134742016 | bytes 10551296 | tf_op jit(solution)/shard_map/brm,bmd->brd/dot_general | solution.py:81
  272.4 1.2 copy.43
  273.6 1.2 convolution_convert_fusion
  275.4 1.0 slice.16
  277.3 7.2 %all_gather.19 = bf16[60,16,256]{2,1,0:T(8,128)(2,1)S(1)} all-gather(bf16[15,16,256]{2,1,0:T(8,128)(2,1)S(1)} %slice.17), channel_id=1, replica_groups=mesh['parts'=2,'dp'=4,'tensor'=4] {'dp'}, dimensions={0}, use_global_device_ids=true | all-gather | bytes 614400 | tf_op jit(solution)/shard_map/all_gather | solution.py:97
  285.2 3.3 convolution_convert_fusion.5
  288.5 7.5 %copy.38 = bf16[2048,4,256]{2,1,0:T(4,128)(2,1)} copy(bf16[2048,4,256]{0,2,1:T(8,128)(2,1)} %bitcast.76) | data formatting | bytes 8388608
  295.9 13.4 %all-gather.8.cloned.1.call-done = bf16[60,16,2048]{2,1,0:T(8,128)(2,1)} async-done(((bf16[15,16,2048]{2,1,0:T(8,128)(2,1)}), bf16[60,16,2048]{2,1,0:T(8,128)(2,1)}) %all-gather.8.cloned.1.call-update) | async-done | bytes 3932176 | tf_op jit(solution)/shard_map/all_gather | solution.py:96
  309.3 2.8 gather_fusion.6
  312.7 13.7 %convolution_convert_fusion.1 = bf16[8192,2048]{1,0:T(8,128)(2,1)} fusion(bf16[32,8192]{1,0:T(8,128)(2,1)S(1)} %bitcast.83, bf16[32,2048]{1,0:T(8,128)(2,1)S(1)} %copy-done), kind=kOutput, calls=%fused_computation.9 | convolution fusion | flops 1090519040 | bytes 34209792 | tf_op jit(solution)/shard_map/th,tk->hk/dot_general | solution.py:102
  326.4 55.8 %copy.37 = bf16[2048,4,2048]{2,1,0:T(4,128)(2,1)} copy(bf16[2048,4,2048]{0,2,1:T(8,128)(2,1)} %bitcast.71) | data formatting | bytes 67108864
  (52 shorter events, 5.5 us)
Async XLA Ops:
  7.2 30.1 %copy-start = (bf16[32,2048]{1,0:T(8,128)(2,1)S(1)}, bf16[32,2048]{1,0:T(8,128)(2,1)}, u32[]{:S(2)}) copy-start(bf16[32,2048]{1,0:T(8,128)(2,1)} %param.10) | copy-start | bytes 393220
  7.2 70.0 %all-gather.6.cloned.1.call-start = ((), (), s32[]{:S(2)}) async-start(), calls=%async_computation.3 | async-start | bytes 2621440 | tf_op jit(solution)/shard_map/all_gather | solution.py:48
  37.3 15.3 %copy-start.4 = (s32[64]{0:T(128)S(1)}, s32[64]{0:T(128)}, u32[]{:S(2)}) copy-start(s32[64]{0:T(128)} %param.14) | copy-start | bytes 772
  51.8 62.0 %all-gather.4.cloned.1.call-start = ((), (), s32[]{:S(2)}) async-start(), calls=%async_computation.1 | async-start | bytes 5242880 | tf_op jit(solution)/shard_map/all_gather | solution.py:67
  52.5 98.2 %all-reduce.3.cloned.1.call-start = ((), (), s32[]{:S(2)}) async-start(), calls=%async_computation.4 | async-start | bytes 131072 | tf_op jit(solution)/shard_map/psum | solution.py:65
  87.5 142.5 %reduce-scatter.2.cloned.1.call-start = ((), (), s32[]{:S(2)}) async-start(), calls=%async_computation.2 | async-start | bytes 5242880 | tf_op jit(solution)/shard_map/reduce_scatter | solution.py:69
  127.6 140.1 %all-reduce.5.cloned.1.call-start = ((), (), s32[]{:S(2)}) async-start(), calls=%async_computation.5 | async-start | bytes 131072 | tf_op jit(solution)/shard_map/psum | solution.py:80
  131.1 7.9 %copy-start.1 = (s32[32]{0:T(128)S(1)}, s32[32]{0:T(128)}, u32[]{:S(2)}) copy-start(s32[32]{0:T(128)} %param.15) | copy-start | bytes 388
  131.1 99.0 %copy-start.3 = (bf16[2048,256]{1,0:T(8,128)(2,1)S(1)}, bf16[2048,256]{1,0:T(8,128)(2,1)}, u32[]{:S(2)}) copy-start(bf16[2048,256]{1,0:T(8,128)(2,1)} %param.9) | copy-start | bytes 3145732
  233.1 76.2 %all-gather.8.cloned.1.call-start = ((), (), s32[]{:S(2)}) async-start(), calls=%async_computation.6 | async-start | bytes 4915200 | tf_op jit(solution)/shard_map/all_gather | solution.py:96
  273.6 2.9 copy-start.2
Sparse Core Ops, SparseCore 0:
  51.9 25.2 all-gather.5
  78.8 35.0 all-gather.3
  116.7 33.9 all-reduce.2
  153.6 76.4 reduce-scatter.1
  233.2 34.4 all-reduce.4
  276.6 32.6 all-gather.7
where the time goes:
time: 391 us; the launch traced here: 389 us
  waiting for transfers between devices  188 us (48%)
  local copies, waits for them, and re-layouts  111 us (28%)
  matrix products  61 us (16%)
  between operations  14.4 us (4%)
  blocking collectives  13 us (3%)
    unnamed x20, local copies, waits for them, and re-layouts  98.9 us
    reduce_scatter x1, waiting for transfers between devices, body(): lax.psum_scatter(base_terms.astype(jnp.bfloat16), 'tensor', scatter_dimen...  79.3 us
    psum x1, waiting for transfers between devices, body(): rank_grad = lax.psum(partial_back.astype(jnp.bfloat16), 'tensor')  34.6 us
    all_gather x1, waiting for transfers between devices, body(): lax.all_gather(base_v, 'dp', axis=1, tiled=True)  26.2 us
    all_gather x1, waiting for transfers between devices, body(): lax.all_gather(flat_a, 'dp', axis=1, tiled=True)  22.9 us
    dot_general x1, matrix products, body(): jnp.dot(tokens, lax.all_gather(base_v, 'dp', axis=1, tiled=True), preferr...  13.8 us
    dot_general x1, matrix products, body(): jnp.einsum('th,tk->hk', task_embed, tenant_a.reshape(tenants, rank_part *...  13.7 us
    dot_general x1, matrix products, body(): jnp.dot(task_embed, head_a.reshape(hidden, rank_part * width_part), prefe...  13.6 us
  transfers between devices with their start and end apart: 6, of which 6 were waited for; matrix products, arithmetic and copies ran while one was open for 11% of the time, Pallas kernels for 0%

commit v1 on v0

v1 whole, which is shorter than its diff:
```python
import functools

import jax
import jax.numpy as jnp
from jax import lax
from jax.experimental import pallas as pl
from jax.experimental.pallas import tpu as pltpu
from jax.sharding import PartitionSpec as P

R = 16
BLOCK = 128
SLOTS = 16
STEP = 256
F32 = jnp.float32
BF16 = jnp.bfloat16


def owner_tables(block_tenant, tenants, blocks, groups):
    ids = jnp.arange(tenants, dtype=jnp.int32)
    block_group = jnp.arange(blocks * groups, dtype=jnp.int32) // blocks
    member = block_tenant[None, :] == ids[:, None]
    owner = jnp.max(jnp.where(member, block_group[None, :], -1), axis=1)
    earlier = (owner[None, :] == owner[:, None]) & (ids[None, :] < ids[:, None])
    slot = jnp.sum(earlier.astype(jnp.int32), axis=1)
    group_ids = jnp.arange(groups, dtype=jnp.int32)
    slot_ids = jnp.arange(SLOTS, dtype=jnp.int32)
    place = (owner[None, None, :] == group_ids[:, None, None]) & (
        slot[None, None, :] == slot_ids[None, :, None]
    )
    return place


def dot(a, b):
    return jnp.dot(a, b, preferred_element_type=F32)


def dot_nt(a, b):
    return lax.dot_general(a, b, (((1,), (1,)), ((), ())), preferred_element_type=F32)


def generate_kernel(count, embed_ref, head_ref, out_ref, total):
    step = pl.program_id(0)
    part, ranks, width = head_ref.shape
    rows = embed_ref.shape[0]

    @pl.when(step == 0)
    def _():
        total[...] = jnp.zeros_like(total)

    spread = lax.broadcasted_iota(jnp.int32, (part, part * ranks), 0) == (
        lax.broadcasted_iota(jnp.int32, (part, part * ranks), 1) // ranks
    )
    wide = dot(embed_ref[...], spread.astype(F32).astype(BF16))
    row = lax.broadcasted_iota(jnp.int32, wide.shape, 0)
    col = lax.broadcasted_iota(jnp.int32, wide.shape, 1)
    wide = jnp.where((row // count) % ranks == col % ranks, wide, 0.0).astype(BF16)
    total[...] += dot(wide, head_ref[...].reshape(part * ranks, width))

    @pl.when(step == pl.num_programs(0) - 1)
    def _():
        out_ref[...] = total[...].astype(BF16)


def generate(embed, head, count):
    hidden, ranks, width = head.shape
    rows = embed.shape[0]
    return pl.pallas_call(
        functools.partial(generate_kernel, count),
        grid=(hidden // STEP,),
        in_specs=[
            pl.BlockSpec((rows, STEP), lambda i: (0, i)),
            pl.BlockSpec((STEP, ranks, width), lambda i: (i, 0, 0)),
        ],
        out_specs=pl.BlockSpec((rows, width), lambda i: (0, 0)),
        out_shape=jax.ShapeDtypeStruct((rows, width), BF16),
        scratch_shapes=[pltpu.VMEM((rows, width), F32)],
        compiler_params=pltpu.CompilerParams(vmem_limit_bytes=40 * 2**20),
        cost_estimate=pl.CostEstimate(
            flops=2 * rows * hidden * ranks * width,
            bytes_accessed=2 * hidden * ranks * width,
            transcendentals=0,
        ),
    )(embed, head)


def head_grad_kernel(embed_ref, grad_ref, out_ref):
    part, ranks, width = out_ref.shape
    spread = (
        lax.broadcasted_iota(jnp.int32, (part * ranks, part), 0) // ranks
    ) == lax.broadcasted_iota(jnp.int32, (part * ranks, part), 1)
    wide = dot(spread.astype(F32).astype(BF16), embed_ref[...])
    row = lax.broadcasted_iota(jnp.int32, wide.shape, 0)
    col = lax.broadcasted_iota(jnp.int32, wide.shape, 1)
    wide = jnp.where((col // SLOTS) % ranks == row % ranks, wide, 0.0).astype(BF16)
    out = dot(wide, grad_ref[...]).astype(BF16)
    out_ref[...] = out.reshape(part, ranks, width)


def head_grad(embed, grad, ranks):
    hidden, depth = embed.shape
    width = grad.shape[1]
    return pl.pallas_call(
        head_grad_kernel,
        grid=(hidden // STEP,),
        in_specs=[
            pl.BlockSpec((STEP, depth), lambda i: (i, 0)),
            pl.BlockSpec((depth, width), lambda i: (0, 0)),
        ],
        out_specs=pl.BlockSpec((STEP, ranks, width), lambda i: (i, 0, 0)),
        out_shape=jax.ShapeDtypeStruct((hidden, ranks, width), BF16),
        compiler_params=pltpu.CompilerParams(vmem_limit_bytes=40 * 2**20),
        cost_estimate=pl.CostEstimate(
            flops=2 * hidden * ranks * depth * width,
            bytes_accessed=2 * hidden * ranks * width,
            transcendentals=0,
        ),
    )(embed, grad)


def body(tokens, target, task_embed, head_a, head_b, base_v, block_tenant, block_count):
    groups = lax.axis_size("dp")
    group_now = lax.axis_index("dp")
    tenants, hidden = task_embed.shape
    rank_part = head_a.shape[1]
    width = head_a.shape[2]
    kv_part = head_b.shape[2]
    rows = tokens.shape[0]
    blocks = rows // BLOCK

    every_v = lax.all_gather(base_v, "dp", axis=0)

    embed_rows = jnp.tile(task_embed, (rank_part, 1))
    flat_b = generate(embed_rows, head_b, tenants)
    every_b = lax.all_gather(flat_b, ("dp", "tensor"), axis=0)

    place = owner_tables(block_tenant, tenants, blocks, groups)
    place_bf = place.astype(BF16)
    slot_rows = dot(place_bf.reshape(groups * SLOTS, tenants), task_embed).astype(BF16)
    slot_rows = jnp.broadcast_to(
        slot_rows.reshape(groups, 1, SLOTS, hidden), (groups, rank_part, SLOTS, hidden)
    ).reshape(groups * rank_part * SLOTS, hidden)
    slot_cols = slot_rows.T

    flat_a = generate(slot_rows, head_a, SLOTS)
    own_a = lax.all_to_all(
        flat_a.reshape(groups, rank_part * SLOTS, width), "dp", 0, 0, tiled=True
    ).reshape(R * SLOTS, width)

    mine = lax.dynamic_index_in_dim(place_bf, group_now, 0, keepdims=False)
    shards = every_b.shape[0] // groups
    every_b = every_b.reshape(groups, shards, rank_part, tenants, kv_part)
    own_b = jnp.einsum("st,dxrtc->drsxc", mine, every_b, preferred_element_type=F32)
    own_b = own_b.astype(BF16).reshape(R, SLOTS, shards * kv_part)
    kv = shards * kv_part
    own_b_cols = lax.dynamic_slice_in_dim(own_b, lax.axis_index("tensor") * kv_part, kv_part, 2)
    own_b_cols = own_b_cols.reshape(R * SLOTS, kv_part)
    flat_own_b = own_b.reshape(R * SLOTS, kv)
    full_v = jnp.transpose(every_v, (1, 0, 2)).reshape(width, kv)
    gram_b = jnp.einsum("rsc,qsc->srq", own_b, own_b, preferred_element_type=F32)
    through = dot_nt(flat_own_b, full_v).astype(BF16)

    own_blocks = lax.dynamic_slice_in_dim(block_tenant, group_now * blocks, blocks)
    tenant_hot = own_blocks[:, None] == jnp.arange(tenants, dtype=jnp.int32)[None, :]
    pick = jnp.sum(
        (mine.astype(F32)[:, None, :] * tenant_hot[None, :, :].astype(F32)), axis=2
    )
    count = block_count.astype(F32)
    slot_count = jnp.sum(mine.astype(F32) * count[None, :], axis=1)
    slot_weight = 1.0 / (BLOCK * jnp.maximum(slot_count, 1.0))
    block_weight = 1.0 / (BLOCK * jnp.sum(jnp.where(tenant_hot, count[None, :], 0.0), axis=1))

    pick_rows = jnp.repeat(pick, BLOCK, axis=1)
    partial_l = dot_nt(own_a, tokens).reshape(R, SLOTS, rows)
    partial_z = (dot_nt(through, tokens) - dot_nt(own_b_cols, target)).reshape(R, SLOTS, rows)
    partial_l = jnp.sum(partial_l * pick_rows[None], axis=1)
    partial_z = jnp.sum(partial_z * pick_rows[None], axis=1)
    both = jnp.concatenate([partial_l, partial_z], axis=0).astype(BF16)
    both = lax.psum(both, "tensor")
    low_rank = both[:R]
    back = both[R:].astype(F32).reshape(R, blocks, BLOCK)
    low_blocks = low_rank.reshape(R, blocks, BLOCK)
    gram_block = jnp.einsum(
        "sb,srq->brq", pick, gram_b, precision=lax.Precision.HIGHEST
    )
    cross = jnp.einsum(
        "brq,qbm->rbm", gram_block.astype(BF16), low_blocks, preferred_element_type=F32
    )
    rank_grad = (back + 2.0 * cross) * block_weight[None, :, None]
    rank_grad = rank_grad.astype(BF16).reshape(R, rows)

    pick_bf = pick_rows.astype(BF16)
    spread_g = (rank_grad[:, None, :] * pick_bf[None]).reshape(R * SLOTS, rows)
    spread_l = (low_rank[:, None, :] * pick_bf[None]).reshape(R * SLOTS, rows)
    grad_a = (2.0 * dot(spread_g, tokens)).astype(BF16)
    every_a = lax.all_to_all(
        grad_a.reshape(groups, rank_part * SLOTS, width), "dp", 0, 0, tiled=True
    ).reshape(groups * rank_part * SLOTS, width)

    low_x = dot(spread_l, tokens).astype(BF16)
    grad_b = dot(low_x, full_v).astype(BF16)
    grad_b = lax.psum_scatter(grad_b, "tensor", scatter_dimension=1, tiled=True).astype(F32)
    gram_l = jnp.einsum("rbm,qbm->brq", low_blocks, low_blocks, preferred_element_type=F32)
    gram_l = jnp.einsum("sb,brq->srq", pick, gram_l, precision=lax.Precision.HIGHEST)
    adapted = jnp.einsum(
        "srq,qsc->rsc",
        gram_l.astype(BF16),
        own_b_cols.reshape(R, SLOTS, kv_part),
        preferred_element_type=F32,
    )
    grad_b = grad_b - dot(spread_l, target)
    grad_b = grad_b.reshape(R, SLOTS, kv_part) + 2.0 * adapted
    grad_b = (2.0 * grad_b * slot_weight[None, :, None]).astype(BF16)
    every_gb = lax.all_to_all(
        grad_b.reshape(groups, rank_part * SLOTS, kv_part), "dp", 0, 0, tiled=True
    ).reshape(groups * rank_part * SLOTS, kv_part)

    grad_head_b = head_grad(slot_cols, every_gb, rank_part)
    grad_head_a = head_grad(slot_cols, every_a, rank_part)
    return (grad_head_a, grad_head_b)


def solution(mesh):
    return jax.shard_map(
        body,
        mesh=mesh,
        in_specs=(
            P(("parts", "dp"), "tensor"),
            P(("parts", "dp"), "tensor"),
            P("parts", None),
            P(None, "dp", "tensor"),
            P(None, "dp", "tensor"),
            P("tensor", "dp"),
            P("parts"),
            P("parts"),
        ),
        out_specs=(P("parts", "dp", "tensor"), P("parts", "dp", "tensor")),
        check_vma=False,
    )
```

time: 391 us -> 214 us (0.55)
  waiting for transfers between devices: 188 us -> 86.8 us
  local copies, waits for them, and re-layouts: 111 us -> 13.7 us
  Pallas kernels: 0 us -> 42.8 us
  matrix products: 61 us -> 40.4 us
  blocking collectives: 13 us -> 0 us
  starting transfers between devices: 0.42 us -> 11.6 us
    unnamed x20 -> x21, local copies, waits for them, and re-layouts: 98.9 us -> 3.83 us
    reduce_scatter x1, waiting for transfers between devices: 79.3 us -> 10.4 us  [body(): lax.psum_scatter(grad_b, 'tensor', scatter_dimension=1, tiled=True)]
    pallas_call x0 -> x4, Pallas kernels: none -> 42.8 us  [the longest x2 21.6 us: generate(): pl.pallas_call(functools.partial(generate_kernel, count), grid=(hidden //...]
    all_gather x3 -> x2, waiting for transfers between devices: 62.5 us -> 24.6 us  [the longest x1 24.6 us: body(): every_v = lax.all_gather(base_v, 'dp', axis=0)]
    dot_general x12 -> x14, matrix products: 61 us -> 40.4 us  [the longest x3 18.6 us: dot_nt(): lax.dot_general(a, b, (((1,), (1,)), ((), ())), preferred_element_type=F32)]
    all_to_all x0 -> x3, waiting for transfers between devices: none -> 17 us  [the longest x1 16 us: body(): lax.all_to_all(flat_a.reshape(groups, rank_part * SLOTS, width), 'dp', 0,...]
    all_gather x2 -> x0, blocking collectives: 13 us -> none  [the longest x1 7.19 us: body(): lax.all_gather(grad_b.reshape(TCAP, R, kv_part), 'dp', axis=0, tiled=True)]
    psum x2 -> x1, waiting for transfers between devices: 45.6 us -> 34 us  [body(): both = lax.psum(both, 'tensor')]
  transfers between devices with their start and end apart: 6 -> 7, of which waited for: 6 -> 5; matrix products, arithmetic and copies ran while one was open for 11% -> 11% of each run, Pallas kernels for 0% -> 15%
where the time goes in v1:
time: 214 us
  waiting for transfers between devices  86.8 us (41%)
  Pallas kernels  42.8 us (20%)
  matrix products  40.4 us (19%)
  between operations  14.1 us (7%)
  local copies, waits for them, and re-layouts  13.7 us (6%)
  starting transfers between devices  11.6 us (5%)
  other arithmetic  4.25 us (2%)
    psum x1, waiting for transfers between devices, body(): both = lax.psum(both, 'tensor')  34 us
    all_gather x1, waiting for transfers between devices, body(): every_v = lax.all_gather(base_v, 'dp', axis=0)  24.6 us
    pallas_call x2, Pallas kernels, generate(): pl.pallas_call(functools.partial(generate_kernel, count), grid=(hidden //...  21.6 us
    pallas_call x2, Pallas kernels, head_grad(): pl.pallas_call(head_grad_kernel, grid=(hidden // STEP,), in_specs=[pl.Blo...  21.1 us
    dot_general x3, matrix products, dot_nt(): lax.dot_general(a, b, (((1,), (1,)), ((), ())), preferred_element_type=F32)  18.6 us
    dot_general x4, matrix products, dot(): return jnp.dot(a, b, preferred_element_type=F32)  18.1 us
    all_to_all x1, waiting for transfers between devices, body(): lax.all_to_all(flat_a.reshape(groups, rank_part * SLOTS, width), 'dp', 0,...  16 us
    reduce_scatter x1, waiting for transfers between devices, body(): lax.psum_scatter(grad_b, 'tensor', scatter_dimension=1, tiled=True)  10.4 us
  transfers between devices with their start and end apart: 7, of which 5 were waited for; matrix products, arithmetic and copies ran while one was open for 11% of the time, Pallas kernels for 15%

profile of v1, /device:TPU:0, one launch (start us, length us, event | category | flops | bytes accessed | tf_op | source)
XLA Modules:
  0.0 213.6 jit_solution(5682004753317765226)
XLA Ops:
  7.2 1.0 tile.4
  8.3 2.2 %copy-done.1 = bf16[2048,4,256]{2,1,0:T(4,128)(2,1)S(1)} copy-done((bf16[2048,4,256]{2,1,0:T(4,128)(2,1)S(1)}, bf16[2048,4,256]{2,1,0:T(4,128)(2,1)}, u32[]{:S(2)}) %copy-start.1) | copy-done | bytes 4194328
  10.5 3.9 %shard_map.96 = bf16[128,256]{1,0:T(8,128)(2,1)} custom-call(bf16[128,2048]{1,0:T(8,128)(2,1)S(1)} %bitcast.117, bf16[2048,4,256]{2,1,0:T(4,128)(2,1)S(1)} %copy-done.1), custom_call_target="tpu_custom_call" | custom-call | flops 536870912 | bytes 4194304 | tf_op jit(solution)/shard_map/pallas_call | solution.py:67
  14.5 0.7 all-gather.7.cloned.1.call-update
  15.9 17.7 %shard_map.95 = bf16[256,2048]{1,0:T(8,128)(2,1)} custom-call(bf16[256,2048]{1,0:T(8,128)(2,1)S(1)} %bitcast.112, bf16[2048,4,2048]{2,1,0:T(4,128)(2,1)} %head_ref.2), custom_call_target="tpu_custom_call" | custom-call | flops 8589934592 | bytes 33554432 | tf_op jit(solution)/shard_map/pallas_call | solution.py:67
  33.6 4.4 %all-to-all-start = ((bf16[4,64,2048]{2,1,0:T(8,128)(2,1)}), bf16[4,64,2048]{2,1,0:T(8,128)(2,1)}, u32[]{:S(2)}, u32[]{:S(2)}) async-start(bf16[4,64,2048]{2,1,0:T(8,128)(2,1)} %bitcast.4), calls=%async_computation | async-start | bytes 2097152 | tf_op jit(solution)/shard_map/all_to_all | solution.py:145
  38.4 0.7 copy.97
  39.1 0.5 copy.43
  39.9 16.0 %all-to-all-done = bf16[4,64,2048]{2,1,0:T(8,128)(2,1)} async-done(((bf16[4,64,2048]{2,1,0:T(8,128)(2,1)}), bf16[4,64,2048]{2,1,0:T(8,128)(2,1)}, u32[]{:S(2)}, u32[]{:S(2)}) %all-to-all-start) | async-done | bytes 1048608 | tf_op jit(solution)/shard_map/all_to_all | solution.py:145
  55.9 6.9 %fusion.6 = bf16[16,2048]{1,0:T(8,128)(2,1)} fusion(bf16[16,16,2048]{2,1,0:T(8,128)(2,1)} %bitcast.5, bf16[2048,2048]{1,0:T(8,128)(2,1)} %param.8, f32[16,2048]{1,0:T(8,128)S(1)} %bitcast.133), kind=kOutput, calls=%fused_computation.10 | convolution fusion | flops 2148499456 | bytes 9633792 | tf_op jit(solution)/shard_map/dot_general | solution.py:38
  62.8 1.6 fusion.9
  64.4 0.4 copy.44
  65.6 0.9 copy.70
  66.5 1.1 fusion.39
  67.5 24.6 %all-gather.7.cloned.1.call-done = bf16[8192,256]{1,0:T(8,128)(2,1)} async-done(((bf16[2048,256]{1,0:T(8,128)(2,1)}), bf16[8192,256]{1,0:T(8,128)(2,1)}) %all-gather.7.cloned.1.call-update) | async-done | bytes 4194320 | tf_op jit(solution)/shard_map/all_gather | solution.py:130
  92.1 6.2 %copy.45 = bf16[2048,4,256]{0,2,1:T(8,128)(2,1)} copy(bf16[2048,4,256]{2,0,1:T(8,128)(2,1)} %bitcast.120) | data formatting | bytes 8388608 | tf_op jit(solution)/shard_map/transpose | solution.py:158
  98.4 9.4 %fusion.19 = f32[256,2048]{1,0:T(8,128)} fusion(bf16[2048,2048]{1,0:T(8,128)(2,1)} %param.8, bf16[256,1024]{1,0:T(8,128)(2,1)S(1)} %bitcast.132, bf16[2048,1024]{0,1:T(8,128)(2,1)} %bitcast.121), kind=kOutput, calls=%fused_computation.28 | convolution fusion | flops 3221749760 | bytes 15204352 | tf_op jit(solution)/shard_map/dot_general | solution.py:38
  107.8 2.2 %multiply_reduce_fusion = bf16[16,2048]{1,0:T(8,128)(2,1)S(1)} fusion(f32[16,2048]{1,0:T(8,128)S(1)} %bitcast.134, f32[256,2048]{1,0:T(8,128)} %fusion.19, bf16[256,256]{1,0:T(8,128)(2,1)S(1)} %bitcast.135, bf16[2048,256]{1,0:T(8,128)(2,1)S(1)} %copy-done), kind=kOutput, calls=%fused_computation.9 | convolution fusion | flops 269975552 | bytes 3473408 | tf_op jit(solution)/shard_map/dot_general | solution.py:38
  110.0 0.7 pad_maximum_fusion
  111.3 34.0 %all-reduce.2.cloned.1.call-done = bf16[32,2048]{1,0:T(8,128)(2,1)} async-done(((bf16[32,2048]{1,0:T(8,128)(2,1)}), bf16[32,2048]{1,0:T(8,128)(2,1)}) %all-reduce.2.cloned.1.call-update) | async-done | bytes 131088 | tf_op jit(solution)/shard_map/psum | solution.py:178
  145.3 0.9 fusion.41
  146.4 2.0 broadcast_multiply_fusion
  148.4 9.2 %convolution_convert_fusion.3 = bf16[256,1024]{1,0:T(8,128)(2,1)} fusion(bf16[2048,1024]{0,1:T(8,128)(2,1)} %bitcast.122, bf16[256,2048]{1,0:T(8,128)(2,1)S(1)} %bitcast.123, bf16[2048,2048]{1,0:T(8,128)(2,1)} %param.8), kind=kOutput, calls=%fused_computation.11 | convolution fusion | flops 3222011904 | bytes 14155776 | tf_op jit(solution)/shard_map/dot_general | solution.py:34
  157.6 7.0 %fusion.5 = bf16[256,2048]{1,0:T(8,128)(2,1)} fusion(bf16[256,2048]{1,0:T(8,128)(2,1)} %bitcast.131, bf16[2048,2048]{1,0:T(8,128)(2,1)} %param.8), kind=kOutput, calls=%fused_computation.5 | convolution fusion | flops 2148532224 | bytes 10485760 | tf_op jit(solution)/shard_map/dot_general | solution.py:34
  164.6 3.5 %all-to-all-start.1 = ((bf16[4,64,2048]{2,1,0:T(8,128)(2,1)}), bf16[4,64,2048]{2,1,0:T(8,128)(2,1)S(1)}, u32[]{:S(2)}, u32[]{:S(2)}) async-start(bf16[4,64,2048]{2,1,0:T(8,128)(2,1)} %bitcast.130), calls=%async_computation.1 | async-start | bytes 2097152 | tf_op jit(solution)/shard_map/all_to_all | solution.py:195
  168.6 10.4 %reduce-scatter.2.cloned.1.call-done = bf16[256,256]{1,0:T(8,128)(2,1)} async-done(((bf16[256,1024]{1,0:T(8,128)(2,1)}), bf16[256,256]{1,0:T(8,128)(2,1)}) %reduce-scatter.2.cloned.1.call-update) | async-done | bytes 131088 | tf_op jit(solution)/shard_map/reduce_scatter | solution.py:201
  179.0 1.7 convolution_subtract_fusion.1
  180.9 0.7 copy.62
  181.6 1.0 all-to-all-done.1
  182.6 3.3 %all-to-all-start.2 = ((bf16[4,64,256]{2,1,0:T(8,128)(2,1)}), bf16[4,64,256]{2,1,0:T(8,128)(2,1)S(1)}, u32[]{:S(2)}, u32[]{:S(2)}) async-start(bf16[4,64,256]{2,1,0:T(8,128)(2,1)} %bitcast.29), calls=%async_computation.3 | async-start | bytes 262144 | tf_op jit(solution)/shard_map/all_to_all | solution.py:213
  185.9 15.2 %shard_map.97 = bf16[2048,4,2048]{2,1,0:T(4,128)(2,1)} custom-call(bf16[2048,256]{1,0:T(8,128)(2,1)S(1)} %bitcast.114, bf16[256,2048]{1,0:T(8,128)(2,1)S(1)} %bitcast.116), custom_call_target="tpu_custom_call" | custom-call | flops 8589934592 | bytes 33554432 | tf_op jit(solution)/shard_map/pallas_call | solution.py:102
  201.1 5.9 %shard_map.98 = bf16[2048,4,256]{2,1,0:T(4,128)(2,1)} custom-call(bf16[2048,256]{1,0:T(8,128)(2,1)S(1)} %bitcast.115, bf16[256,256]{1,0:T(8,128)(2,1)S(1)} %bitcast.118), custom_call_target="tpu_custom_call" | custom-call | flops 1073741824 | bytes 4194304 | tf_op jit(solution)/shard_map/pallas_call | solution.py:102
  (54 shorter events, 3.5 us)
Async XLA Ops:
  7.2 100.6 %copy-start = (bf16[2048,256]{1,0:T(8,128)(2,1)S(1)}, bf16[2048,256]{1,0:T(8,128)(2,1)}, u32[]{:S(2)}) copy-start(bf16[2048,256]{1,0:T(8,128)(2,1)} %param.9) | copy-start | bytes 3145732
  7.2 8.4 %copy-start.3 = (bf16[32,2048]{1,0:T(8,128)(2,1)S(1)}, bf16[32,2048]{1,0:T(8,128)(2,1)}, u32[]{:S(2)}) copy-start(bf16[32,2048]{1,0:T(8,128)(2,1)} %param.10) | copy-start | bytes 393220
  7.2 8.0 %copy-start.7 = (s32[64]{0:T(128)S(1)}, s32[64]{0:T(128)}, u32[]{:S(2)}) copy-start(s32[64]{0:T(128)} %param.14) | copy-start | bytes 772
  7.2 55.6 %all-gather.5.cloned.1.call-start = ((), (), s32[]{:S(2)}) async-start(), calls=%async_computation.6 | async-start | bytes 1114112 | tf_op jit(solution)/shard_map/all_gather | solution.py:134
  8.3 2.2 %copy-start.1 = (bf16[2048,4,256]{2,1,0:T(4,128)(2,1)S(1)}, bf16[2048,4,256]{2,1,0:T(4,128)(2,1)}, u32[]{:S(2)}) copy-start(bf16[2048,4,256]{2,1,0:T(4,128)(2,1)} %head_ref.3) | copy-start | bytes 12582916
  14.4 77.7 %all-gather.7.cloned.1.call-start = ((), (), s32[]{:S(2)}) async-start(), calls=%async_computation.7 | async-start | bytes 5242880 | tf_op jit(solution)/shard_map/all_gather | solution.py:130
  33.6 6.1 %copy-start.8 = (s32[32]{0:T(128)S(1)}, s32[32]{0:T(128)}, u32[]{:S(2)}) copy-start(s32[32]{0:T(128)} %param.15) | copy-start | bytes 388
  33.6 22.3 %all-to-all-start = ((bf16[4,64,2048]{2,1,0:T(8,128)(2,1)}), bf16[4,64,2048]{2,1,0:T(8,128)(2,1)}, u32[]{:S(2)}, u32[]{:S(2)}) async-start(bf16[4,64,2048]{2,1,0:T(8,128)(2,1)} %bitcast.4), calls=%async_computation | async-start | bytes 2097152 | tf_op jit(solution)/shard_map/all_to_all | solution.py:145
  38.0 107.4 %all-reduce.2.cloned.1.call-start = ((), (), s32[]{:S(2)}) async-start(), calls=%async_computation.4 | async-start | bytes 262144 | tf_op jit(solution)/shard_map/psum | solution.py:178
  92.1 6.3 %copy-start.4 = (bf16[32,8,4,256]{3,1,2,0:T(8,128)(2,1)S(1)}, bf16[32,8,4,256]{3,1,2,0:T(8,128)(2,1)}, u32[]{:S(2)}) copy-start(bf16[32,8,4,256]{3,1,2,0:T(8,128)(2,1)} %copy.70) | copy-start | bytes 1572868
  98.3 11.7 %copy-start.6 = (bf16[16,2048]{1,0:T(8,128)(2,1)S(1)}, bf16[16,2048]{1,0:T(8,128)(2,1)}, u32[]{:S(2)}) copy-start(bf16[16,2048]{1,0:T(8,128)(2,1)} %fusion.6) | copy-start | bytes 196612
  98.3 12.6 %copy-start.5 = (f32[16,16,16]{2,1,0:T(8,128)S(1)}, f32[16,16,16]{2,1,0:T(8,128)}, u32[]{:S(2)}) copy-start(f32[16,16,16]{2,1,0:T(8,128)} %fusion.39) | copy-start | bytes 49156
  110.7 68.3 %reduce-scatter.2.cloned.1.call-start = ((), (), s32[]{:S(2)}) async-start(), calls=%async_computation.5 | async-start | bytes 655360 | tf_op jit(solution)/shard_map/reduce_scatter | solution.py:201
  148.4 9.2 %copy-start.2 = (bf16[16,16,2048]{2,1,0:T(8,128)(2,1)}, bf16[16,16,2048]{2,1,0:T(8,128)(2,1)S(1)}, u32[]{:S(2)}) copy-start(bf16[16,16,2048]{2,1,0:T(8,128)(2,1)S(1)} %get-tuple-element.7) | copy-start | bytes 3145732
  164.6 18.0 %all-to-all-start.1 = ((bf16[4,64,2048]{2,1,0:T(8,128)(2,1)}), bf16[4,64,2048]{2,1,0:T(8,128)(2,1)S(1)}, u32[]{:S(2)}, u32[]{:S(2)}) async-start(bf16[4,64,2048]{2,1,0:T(8,128)(2,1)} %bitcast.130), calls=%async_computation.1 | async-start | bytes 2097152 | tf_op jit(solution)/shard_map/all_to_all | solution.py:195
  182.6 18.6 %all-to-all-start.2 = ((bf16[4,64,256]{2,1,0:T(8,128)(2,1)}), bf16[4,64,256]{2,1,0:T(8,128)(2,1)S(1)}, u32[]{:S(2)}, u32[]{:S(2)}) async-start(bf16[4,64,256]{2,1,0:T(8,128)(2,1)} %bitcast.29), calls=%async_computation.3 | async-start | bytes 262144 | tf_op jit(solution)/shard_map/all_to_all | solution.py:213
Sparse Core Ops, SparseCore 0:
  14.5 42.4 all-gather.4
  58.6 33.4 all-gather.6
  110.8 34.4 all-reduce.1
  157.7 21.2 reduce-scatter.1

commit v2 on v1

--- a/solution.py
+++ b/solution.py
@@ -83,27 +83,49 @@
     )(embed, head)
 
 
-def head_grad_kernel(embed_ref, grad_ref, out_ref):
-    part, ranks, width = out_ref.shape
+def spread_kernel(ranks, embed_ref, out_ref):
+    part, depth = embed_ref.shape
     spread = (
         lax.broadcasted_iota(jnp.int32, (part * ranks, part), 0) // ranks
     ) == lax.broadcasted_iota(jnp.int32, (part * ranks, part), 1)
     wide = dot(spread.astype(F32).astype(BF16), embed_ref[...])
     row = lax.broadcasted_iota(jnp.int32, wide.shape, 0)
     col = lax.broadcasted_iota(jnp.int32, wide.shape, 1)
-    wide = jnp.where((col // SLOTS) % ranks == row % ranks, wide, 0.0).astype(BF16)
-    out = dot(wide, grad_ref[...]).astype(BF16)
+    out_ref[...] = jnp.where((col // SLOTS) % ranks == row % ranks, wide, 0.0).astype(BF16)
+
+
+def spread_embed(embed, ranks):
+    hidden, depth = embed.shape
+    return pl.pallas_call(
+        functools.partial(spread_kernel, ranks),
+        grid=(hidden // STEP,),
+        in_specs=[pl.BlockSpec((STEP, depth), lambda i: (i, 0))],
+        out_specs=pl.BlockSpec((STEP * ranks, depth), lambda i: (i, 0)),
+        out_shape=jax.ShapeDtypeStruct((hidden * ranks, depth), BF16),
+        compiler_params=pltpu.CompilerParams(vmem_limit_bytes=24 * 2**20),
+        cost_estimate=pl.CostEstimate(
+            flops=2 * hidden * ranks * depth * STEP,
+            bytes_accessed=2 * hidden * ranks * depth,
+            transcendentals=0,
+        ),
+    )(embed)
+
+
+def head_grad_kernel(wide_ref, grad_ref, out_ref):
+    part, ranks, width = out_ref.shape
+    out = dot(wide_ref[...], grad_ref[...]).astype(BF16)
     out_ref[...] = out.reshape(part, ranks, width)
 
 
-def head_grad(embed, grad, ranks):
-    hidden, depth = embed.shape
+def head_grad(wide, grad, ranks):
+    depth = wide.shape[1]
+    hidden = wide.shape[0] // ranks
     width = grad.shape[1]
     return pl.pallas_call(
         head_grad_kernel,
         grid=(hidden // STEP,),
         in_specs=[
-            pl.BlockSpec((STEP, depth), lambda i: (i, 0)),
+            pl.BlockSpec((STEP * ranks, depth), lambda i: (i, 0)),
             pl.BlockSpec((depth, width), lambda i: (0, 0)),
         ],
         out_specs=pl.BlockSpec((STEP, ranks, width), lambda i: (i, 0, 0)),
@@ -114,7 +136,12 @@
             bytes_accessed=2 * hidden * ranks * width,
             transcendentals=0,
         ),
-    )(embed, grad)
+    )(wide, grad)
+
+
+def gather_all(x, axis):
+    shards = lax.axis_size(axis)
+    return lax.all_to_all(jnp.broadcast_to(x[None], (shards,) + x.shape), axis, 0, 0, tiled=True)
 
 
 def body(tokens, target, task_embed, head_a, head_b, base_v, block_tenant, block_count):
@@ -127,11 +154,10 @@
     rows = tokens.shape[0]
     blocks = rows // BLOCK
 
-    every_v = lax.all_gather(base_v, "dp", axis=0)
-
-    embed_rows = jnp.tile(task_embed, (rank_part, 1))
-    flat_b = generate(embed_rows, head_b, tenants)
-    every_b = lax.all_gather(flat_b, ("dp", "tensor"), axis=0)
+    shards = lax.axis_size("tensor")
+    shard_now = lax.axis_index("tensor")
+    full_v = lax.all_gather(base_v, "dp", axis=1, tiled=True)
+    kv = full_v.shape[1]
 
     place = owner_tables(block_tenant, tenants, blocks, groups)
     place_bf = place.astype(BF16)
@@ -139,23 +165,20 @@
     slot_rows = jnp.broadcast_to(
         slot_rows.reshape(groups, 1, SLOTS, hidden), (groups, rank_part, SLOTS, hidden)
     ).reshape(groups * rank_part * SLOTS, hidden)
-    slot_cols = slot_rows.T
-
+
+    flat_b = generate(slot_rows, head_b, SLOTS)
+    own_b_cols = lax.all_to_all(
+        flat_b.reshape(groups, rank_part * SLOTS, kv_part), "dp", 0, 0, tiled=True
+    ).reshape(R * SLOTS, kv_part)
+    every_b = gather_all(own_b_cols, "tensor")
     flat_a = generate(slot_rows, head_a, SLOTS)
     own_a = lax.all_to_all(
         flat_a.reshape(groups, rank_part * SLOTS, width), "dp", 0, 0, tiled=True
     ).reshape(R * SLOTS, width)
 
     mine = lax.dynamic_index_in_dim(place_bf, group_now, 0, keepdims=False)
-    shards = every_b.shape[0] // groups
-    every_b = every_b.reshape(groups, shards, rank_part, tenants, kv_part)
-    own_b = jnp.einsum("st,dxrtc->drsxc", mine, every_b, preferred_element_type=F32)
-    own_b = own_b.astype(BF16).reshape(R, SLOTS, shards * kv_part)
-    kv = shards * kv_part
-    own_b_cols = lax.dynamic_slice_in_dim(own_b, lax.axis_index("tensor") * kv_part, kv_part, 2)
-    own_b_cols = own_b_cols.reshape(R * SLOTS, kv_part)
-    flat_own_b = own_b.reshape(R * SLOTS, kv)
-    full_v = jnp.transpose(every_v, (1, 0, 2)).reshape(width, kv)
+    flat_own_b = jnp.transpose(every_b, (1, 0, 2)).reshape(R * SLOTS, kv)
+    own_b = flat_own_b.reshape(R, SLOTS, kv)
     gram_b = jnp.einsum("rsc,qsc->srq", own_b, own_b, preferred_element_type=F32)
     through = dot_nt(flat_own_b, full_v).astype(BF16)
 
@@ -175,9 +198,9 @@
     partial_l = jnp.sum(partial_l * pick_rows[None], axis=1)
     partial_z = jnp.sum(partial_z * pick_rows[None], axis=1)
     both = jnp.concatenate([partial_l, partial_z], axis=0).astype(BF16)
-    both = lax.psum(both, "tensor")
-    low_rank = both[:R]
-    back = both[R:].astype(F32).reshape(R, blocks, BLOCK)
+    both = jnp.sum(gather_all(both, "tensor").astype(F32), axis=0)
+    low_rank = both[:R].astype(BF16)
+    back = both[R:].reshape(R, blocks, BLOCK)
     low_blocks = low_rank.reshape(R, blocks, BLOCK)
     gram_block = jnp.einsum(
         "sb,srq->brq", pick, gram_b, precision=lax.Precision.HIGHEST
@@ -197,8 +220,6 @@
     ).reshape(groups * rank_part * SLOTS, width)
 
     low_x = dot(spread_l, tokens).astype(BF16)
-    grad_b = dot(low_x, full_v).astype(BF16)
-    grad_b = lax.psum_scatter(grad_b, "tensor", scatter_dimension=1, tiled=True).astype(F32)
     gram_l = jnp.einsum("rbm,qbm->brq", low_blocks, low_blocks, preferred_element_type=F32)
     gram_l = jnp.einsum("sb,brq->srq", pick, gram_l, precision=lax.Precision.HIGHEST)
     adapted = jnp.einsum(
@@ -207,15 +228,22 @@
         own_b_cols.reshape(R, SLOTS, kv_part),
         preferred_element_type=F32,
     )
-    grad_b = grad_b - dot(spread_l, target)
-    grad_b = grad_b.reshape(R, SLOTS, kv_part) + 2.0 * adapted
-    grad_b = (2.0 * grad_b * slot_weight[None, :, None]).astype(BF16)
-    every_gb = lax.all_to_all(
-        grad_b.reshape(groups, rank_part * SLOTS, kv_part), "dp", 0, 0, tiled=True
-    ).reshape(groups * rank_part * SLOTS, kv_part)
-
-    grad_head_b = head_grad(slot_cols, every_gb, rank_part)
-    grad_head_a = head_grad(slot_cols, every_a, rank_part)
+    extra = 2.0 * adapted.reshape(R * SLOTS, kv_part) - dot(spread_l, target)
+    here = (jnp.arange(shards) == shard_now).astype(F32)
+    scale = jnp.tile(2.0 * slot_weight, (R,))
+    grad_b = dot(low_x, full_v).reshape(R * SLOTS, shards, kv_part)
+    grad_b = (grad_b + here[None, :, None] * extra[:, None, :]) * scale[:, None, None]
+    grad_b = grad_b.astype(BF16).reshape(groups, rank_part * SLOTS, shards, kv_part)
+    grad_b = jnp.transpose(grad_b, (0, 2, 1, 3))
+    grad_b = grad_b.reshape(groups * shards, rank_part * SLOTS, kv_part)
+    every_gb = lax.all_to_all(grad_b, ("dp", "tensor"), 0, 0, tiled=True)
+    every_gb = every_gb.reshape(groups, shards, rank_part * SLOTS, kv_part).astype(F32)
+    every_gb = jnp.sum(every_gb, axis=1).astype(BF16)
+    every_gb = every_gb.reshape(groups * rank_part * SLOTS, kv_part)
+
+    wide = spread_embed(slot_rows.T, rank_part)
+    grad_head_a = head_grad(wide, every_a, rank_part)
+    grad_head_b = head_grad(wide, every_gb, rank_part)
     return (grad_head_a, grad_head_b)
 
 

time: 214 us -> 179 us (0.84)
  waiting for transfers between devices: 86.8 us -> 33.4 us
  starting transfers between devices: 11.6 us -> 24.3 us
  local copies, waits for them, and re-layouts: 13.7 us -> 16.8 us
  matrix products: 40.4 us -> 38.2 us
    psum x1 -> x0, waiting for transfers between devices: 34 us -> none  [body(): both = lax.psum(both, 'tensor')]
    all_gather x2 -> x1, waiting for transfers between devices: 24.6 us -> 0.01 us  [body(): full_v = lax.all_gather(base_v, 'dp', axis=1, tiled=True)]
    all_to_all x1 -> x4, waiting for transfers between devices: 0.01 us -> 18.2 us  [the longest x2 18.2 us: gather_all(): lax.all_to_all(jnp.broadcast_to(x[None], (shards,) + x.shape), axis, 0, 0...]
    all_to_all x1 -> x4, starting transfers between devices: 3.32 us -> 17.2 us  [the longest x2 8.71 us: gather_all(): lax.all_to_all(jnp.broadcast_to(x[None], (shards,) + x.shape), axis, 0, 0...]
    reduce_scatter x1 -> x0, waiting for transfers between devices: 10.4 us -> none  [body(): lax.psum_scatter(grad_b, 'tensor', scatter_dimension=1, tiled=True)]
    unnamed x21 -> x18, local copies, waits for them, and re-layouts: 3.83 us -> 7.98 us
    transpose x1 -> x2, local copies, waits for them, and re-layouts: 6.25 us -> 2.36 us  [the longest x1 1.31 us: body(): wide = spread_embed(slot_rows.T, rank_part)]
    pallas_call x0 -> x1, Pallas kernels: none -> 2.5 us  [spread_embed(): pl.pallas_call(functools.partial(spread_kernel, ranks), grid=(hidden // S...]
  transfers between devices with their start and end apart: 7 -> 7, of which waited for: 5 -> 3; matrix products, arithmetic and copies ran while one was open for 11% -> 17% of each run, Pallas kernels for 15% -> 22%
where the time goes in v2:
time: 179 us; the launch traced here: 177 us
  Pallas kernels  44.4 us (25%)
  matrix products  38.2 us (21%)
  waiting for transfers between devices  33.4 us (19%)
  starting transfers between devices  24.3 us (14%)
  local copies, waits for them, and re-layouts  16.8 us (9%)
  between operations  14.3 us (8%)
  other arithmetic  6.13 us (3%)
    pallas_call x2, Pallas kernels, generate(): pl.pallas_call(functools.partial(generate_kernel, count), grid=(hidden //...  22.7 us
    pallas_call x2, Pallas kernels, head_grad(): pl.pallas_call(head_grad_kernel, grid=(hidden // STEP,), in_specs=[pl.Blo...  19.2 us
    dot_general x4, matrix products, dot(): return jnp.dot(a, b, preferred_element_type=F32)  18.7 us
    all_to_all x2, waiting for transfers between devices, gather_all(): lax.all_to_all(jnp.broadcast_to(x[None], (shards,) + x.shape), axis, 0, 0...  18.2 us
    dot_general x3, matrix products, dot_nt(): lax.dot_general(a, b, (((1,), (1,)), ((), ())), preferred_element_type=F32)  17.9 us
    all_to_all x1, waiting for transfers between devices, body(): lax.all_to_all(flat_a.reshape(groups, rank_part * SLOTS, width), 'dp', 0,...  14.5 us
    all_to_all x2, starting transfers between devices, gather_all(): lax.all_to_all(jnp.broadcast_to(x[None], (shards,) + x.shape), axis, 0, 0...  8.71 us
    unnamed x18, local copies, waits for them, and re-layouts  7.98 us
  transfers between devices with their start and end apart: 7, of which 3 were waited for; matrix products, arithmetic and copies ran while one was open for 17% of the time, Pallas kernels for 22%

profile of v2, /device:TPU:0, one launch (start us, length us, event | category | flops | bytes accessed | tf_op | source)
XLA Modules:
  0.0 177.5 jit_solution(17186074493701118014)
XLA Ops:
  8.9 1.1 convolution_convert_fusion.2
  10.2 2.2 %copy-done.4 = bf16[2048,4,256]{2,1,0:T(4,128)(2,1)S(1)} copy-done((bf16[2048,4,256]{2,1,0:T(4,128)(2,1)S(1)}, bf16[2048,4,256]{2,1,0:T(4,128)(2,1)}, u32[]{:S(2)}) %copy-start.4) | copy-done | bytes 4194328
  12.3 4.9 %shard_map.97 = bf16[256,256]{1,0:T(8,128)(2,1)} custom-call(bf16[256,2048]{1,0:T(8,128)(2,1)S(1)} %bitcast.102, bf16[2048,4,256]{2,1,0:T(4,128)(2,1)S(1)} %copy-done.4), custom_call_target="tpu_custom_call" | custom-call | flops 1073741824 | bytes 4194304 | tf_op jit(solution)/shard_map/pallas_call | solution.py:67
  17.3 4.2 %all-to-all-start.1 = ((bf16[4,64,256]{2,1,0:T(8,128)(2,1)}), bf16[4,64,256]{2,1,0:T(8,128)(2,1)S(1)}, u32[]{:S(2)}, u32[]{:S(2)}) async-start(bf16[4,64,256]{2,1,0:T(8,128)(2,1)} %bitcast.8), calls=%async_computation.1 | async-start | bytes 262144 | tf_op jit(solution)/shard_map/all_to_all | solution.py:170
  21.5 17.8 %shard_map.96 = bf16[256,2048]{1,0:T(8,128)(2,1)} custom-call(bf16[256,2048]{1,0:T(8,128)(2,1)S(1)} %bitcast.103, bf16[2048,4,2048]{2,1,0:T(4,128)(2,1)} %head_ref.2), custom_call_target="tpu_custom_call" | custom-call | flops 8589934592 | bytes 33554432 | tf_op jit(solution)/shard_map/pallas_call | solution.py:67
  39.3 3.5 %all-to-all-start = ((bf16[4,64,2048]{2,1,0:T(8,128)(2,1)}), bf16[4,64,2048]{2,1,0:T(8,128)(2,1)S(1)}, u32[]{:S(2)}, u32[]{:S(2)}) async-start(bf16[4,64,2048]{2,1,0:T(8,128)(2,1)} %bitcast.4), calls=%async_computation | async-start | bytes 2097152 | tf_op jit(solution)/shard_map/all_to_all | solution.py:175
  43.3 14.5 %all-to-all-done = bf16[4,64,2048]{2,1,0:T(8,128)(2,1)S(1)} async-done(((bf16[4,64,2048]{2,1,0:T(8,128)(2,1)}), bf16[4,64,2048]{2,1,0:T(8,128)(2,1)S(1)}, u32[]{:S(2)}, u32[]{:S(2)}) %all-to-all-start) | async-done | bytes 1048608 | tf_op jit(solution)/shard_map/all_to_all | solution.py:175
  58.9 5.1 %all-to-all-start.2 = ((bf16[4,256,256]{1,2,0:T(8,128)(2,1)}), bf16[4,256,256]{1,2,0:T(8,128)(2,1)S(1)}, u32[]{:S(2)}, u32[]{:S(2)}) async-start(bf16[4,256,256]{1,2,0:T(8,128)(2,1)} %broadcast_in_dim.42), calls=%async_computation.2 | async-start | bytes 1048576 | tf_op jit(solution)/shard_map/all_to_all | solution.py:144
  64.4 6.3 %fusion.6 = bf16[16,2048]{1,0:T(8,128)(2,1)S(1)} fusion(bf16[16,16,2048]{2,1,0:T(8,128)(2,1)} %bitcast.120, bf16[2048,2048]{1,0:T(8,128)(2,1)} %param.8, f32[16,2048]{1,0:T(8,128)S(1)} %bitcast.123), kind=kOutput, calls=%fused_computation.10 | convolution fusion | flops 2148499456 | bytes 9633792 | tf_op jit(solution)/shard_map/dot_general | solution.py:38
  70.7 7.6 %all-to-all-done.2 = bf16[4,256,256]{1,2,0:T(8,128)(2,1)S(1)} async-done(((bf16[4,256,256]{1,2,0:T(8,128)(2,1)}), bf16[4,256,256]{1,2,0:T(8,128)(2,1)S(1)}, u32[]{:S(2)}, u32[]{:S(2)}) %all-to-all-start.2) | async-done | bytes 524320 | tf_op jit(solution)/shard_map/all_to_all | solution.py:144
  78.3 9.4 %fusion.17 = f32[256,2048]{1,0:T(8,128)} fusion(bf16[2048,2048]{1,0:T(8,128)(2,1)} %param.8, bf16[256,1024]{0,1:T(8,128)(2,1)S(1)} %bitcast.110, bf16[2048,1024]{1,0:T(8,128)(2,1)} %all-gather.2.cloned.1.call-done), kind=kOutput, calls=%fused_computation.26 | convolution fusion | flops 3221749760 | bytes 15204352 | tf_op jit(solution)/shard_map/dot_general | solution.py:38
  87.7 2.2 %multiply_reduce_fusion = bf16[16,2048]{1,0:T(8,128)(2,1)S(1)} fusion(f32[16,2048]{1,0:T(8,128)S(1)} %bitcast.124, f32[256,2048]{1,0:T(8,128)} %fusion.17, bf16[256,256]{1,0:T(8,128)(2,1)S(1)} %bitcast.113, bf16[2048,256]{1,0:T(8,128)(2,1)S(1)} %copy-done), kind=kOutput, calls=%fused_computation.9 | convolution fusion | flops 269975552 | bytes 3473408 | tf_op jit(solution)/shard_map/dot_general | solution.py:38
  90.8 3.7 %all-to-all-start.3 = ((bf16[4,32,2048]{2,1,0:T(8,128)(2,1)}), bf16[4,32,2048]{2,1,0:T(8,128)(2,1)S(1)}, u32[]{:S(2)}, u32[]{:S(2)}) async-start(bf16[4,32,2048]{2,1,0:T(8,128)(2,1)} %broadcast_in_dim.43), calls=%async_computation.3 | async-start | bytes 1048576 | tf_op jit(solution)/shard_map/all_to_all | solution.py:144
  94.5 1.1 copy.22
  95.6 1.4 reshape_reshape.6
  97.7 10.6 %all-to-all-done.3 = bf16[4,32,2048]{2,1,0:T(8,128)(2,1)S(1)} async-done(((bf16[4,32,2048]{2,1,0:T(8,128)(2,1)}), bf16[4,32,2048]{2,1,0:T(8,128)(2,1)S(1)}, u32[]{:S(2)}, u32[]{:S(2)}) %all-to-all-start.3) | async-done | bytes 524320 | tf_op jit(solution)/shard_map/all_to_all | solution.py:144
  109.0 1.1 broadcast_multiply_fusion
  110.1 6.7 %fusion.5 = bf16[256,2048]{1,0:T(8,128)(2,1)} fusion(bf16[256,2048]{1,0:T(8,128)(2,1)S(1)} %bitcast.122, bf16[2048,2048]{1,0:T(8,128)(2,1)} %param.8), kind=kOutput, calls=%fused_computation.5 | convolution fusion | flops 2148532224 | bytes 10485760 | tf_op jit(solution)/shard_map/dot_general | solution.py:34
  116.8 3.5 %all-to-all-start.4 = ((bf16[4,64,2048]{2,1,0:T(8,128)(2,1)}), bf16[4,64,2048]{2,1,0:T(8,128)(2,1)S(1)}, u32[]{:S(2)}, u32[]{:S(2)}) async-start(bf16[4,64,2048]{2,1,0:T(8,128)(2,1)} %bitcast.121), calls=%async_computation.4 | async-start | bytes 2097152 | tf_op jit(solution)/shard_map/all_to_all | solution.py:218
  120.4 9.3 %fusion.18 = f32[256,1024]{1,0:T(8,128)} fusion(bf16[2048,1024]{1,0:T(8,128)(2,1)} %all-gather.2.cloned.1.call-done, bf16[256,2048]{1,0:T(8,128)(2,1)} %bitcast.107, bf16[2048,2048]{1,0:T(8,128)(2,1)} %param.8), kind=kOutput, calls=%fused_computation.27 | convolution fusion | flops 3221749760 | bytes 14680064 | tf_op jit(solution)/shard_map/dot_general | solution.py:34
  130.0 2.7 %reshape.213 = f32[4,64,4,256]{3,2,1,0:T(4,128)} reshape(f32[256,1024]{1,0:T(8,128)} %fusion.18) | data formatting | bytes 2097152 | tf_op jit(solution)/shard_map/reshape | solution.py:234
  132.7 1.7 convolution_subtract_fusion.1
  134.3 2.4 %fusion.16 = bf16[4,64,4,256]{3,1,2,0:T(8,128)(2,1)} fusion(f32[4,64,4,256]{3,2,1,0:T(4,128)} %reshape.213, f32[64]{0:T(128)S(1)} %tile.9, f32[4,64,256]{2,1,0:T(8,128)S(1)} %bitcast.117, f32[4]{0:T(128)S(1)} %compare_convert_fusion), kind=kLoop, calls=%fused_computation.24 | loop fusion | flops 1048576 | bytes 1835280 | tf_op jit(solution)/shard_map/convert_element_type | solution.py:236
  136.8 4.3 %all-to-all-start.5 = ((bf16[16,64,256]{2,1,0:T(8,128)(2,1)}), bf16[16,64,256]{2,1,0:T(8,128)(2,1)}, u32[]{:S(2)}, u32[]{:S(2)}) async-start(bf16[16,64,256]{2,1,0:T(8,128)(2,1)} %bitcast.109), calls=%async_computation.5 | async-start | bytes 1048576 | tf_op jit(solution)/shard_map/all_to_all | solution.py:239
  141.1 1.3 copy.20.embed_ref
  142.4 1.2 copy-done.3
  143.6 2.5 %shard_map.95.wide_ref = bf16[8192,256]{1,0:T(8,128)(2,1)S(1)} custom-call(bf16[2048,256]{1,0:T(8,128)(2,1)S(1)} %copy-done.3), custom_call_target="tpu_custom_call" | custom-call | flops 1073741824 | bytes 4194304 | tf_op jit(solution)/shard_map/pallas_call | solution.py:99
  146.1 14.5 %shard_map.98 = bf16[2048,4,2048]{2,1,0:T(4,128)(2,1)} custom-call(bf16[8192,256]{1,0:T(8,128)(2,1)S(1)} %shard_map.95.wide_ref, bf16[256,2048]{1,0:T(8,128)(2,1)S(1)} %bitcast.105), custom_call_target="tpu_custom_call" | custom-call | flops 8589934592 | bytes 33554432 | tf_op jit(solution)/shard_map/pallas_call | solution.py:124
  160.6 2.0 %copy-done.1 = bf16[8192,256]{1,0:T(8,128)(2,1)} copy-done((bf16[8192,256]{1,0:T(8,128)(2,1)}, bf16[8192,256]{1,0:T(8,128)(2,1)S(1)}, u32[]{:S(2)}) %copy-start.1) | copy-done | bytes 4194328
  162.6 1.1 bitcast_reduce_fusion
  163.7 2.2 %copy-done.2 = bf16[8192,256]{1,0:T(8,128)(2,1)S(1)} copy-done((bf16[8192,256]{1,0:T(8,128)(2,1)S(1)}, bf16[8192,256]{1,0:T(8,128)(2,1)}, u32[]{:S(2)}) %copy-start.2) | copy-done | bytes 4194328
  165.9 4.7 %shard_map.99 = bf16[2048,4,256]{2,1,0:T(4,128)(2,1)} custom-call(bf16[8192,256]{1,0:T(8,128)(2,1)S(1)} %copy-done.2, bf16[256,256]{1,0:T(8,128)(2,1)S(1)} %bitcast.106), custom_call_target="tpu_custom_call" | custom-call | flops 1073741824 | bytes 4194304 | tf_op jit(solution)/shard_map/pallas_call | solution.py:124
  (53 shorter events, 6.4 us)
Async XLA Ops:
  7.2 80.6 %copy-start = (bf16[2048,256]{1,0:T(8,128)(2,1)S(1)}, bf16[2048,256]{1,0:T(8,128)(2,1)}, u32[]{:S(2)}) copy-start(bf16[2048,256]{1,0:T(8,128)(2,1)} %param.9) | copy-start | bytes 3145732
  7.2 71.1 %all-gather.2.cloned.1.call-start = ((), (), s32[]{:S(2)}) async-start(), calls=%async_computation.6 | async-start | bytes 5242880 | tf_op jit(solution)/shard_map/all_gather | solution.py:159
  10.2 2.2 %copy-start.4 = (bf16[2048,4,256]{2,1,0:T(4,128)(2,1)S(1)}, bf16[2048,4,256]{2,1,0:T(4,128)(2,1)}, u32[]{:S(2)}) copy-start(bf16[2048,4,256]{2,1,0:T(4,128)(2,1)} %head_ref.3) | copy-start | bytes 12582916
  17.3 22.0 %all-to-all-start.1 = ((bf16[4,64,256]{2,1,0:T(8,128)(2,1)}), bf16[4,64,256]{2,1,0:T(8,128)(2,1)S(1)}, u32[]{:S(2)}, u32[]{:S(2)}) async-start(bf16[4,64,256]{2,1,0:T(8,128)(2,1)} %bitcast.8), calls=%async_computation.1 | async-start | bytes 262144 | tf_op jit(solution)/shard_map/all_to_all | solution.py:170
  21.5 21.3 %copy-start.6 = (s32[64]{0:T(128)S(1)}, s32[64]{0:T(128)}, u32[]{:S(2)}) copy-start(s32[64]{0:T(128)} %param.14) | copy-start | bytes 772
  21.5 21.4 %copy-start.7 = (s32[32]{0:T(128)S(1)}, s32[32]{0:T(128)}, u32[]{:S(2)}) copy-start(s32[32]{0:T(128)} %param.15) | copy-start | bytes 388
  39.3 18.5 %all-to-all-start = ((bf16[4,64,2048]{2,1,0:T(8,128)(2,1)}), bf16[4,64,2048]{2,1,0:T(8,128)(2,1)S(1)}, u32[]{:S(2)}, u32[]{:S(2)}) async-start(bf16[4,64,2048]{2,1,0:T(8,128)(2,1)} %bitcast.4), calls=%async_computation | async-start | bytes 2097152 | tf_op jit(solution)/shard_map/all_to_all | solution.py:175
  57.8 1.1 copy-start.5
  58.9 19.3 %all-to-all-start.2 = ((bf16[4,256,256]{1,2,0:T(8,128)(2,1)}), bf16[4,256,256]{1,2,0:T(8,128)(2,1)S(1)}, u32[]{:S(2)}, u32[]{:S(2)}) async-start(bf16[4,256,256]{1,2,0:T(8,128)(2,1)} %broadcast_in_dim.42), calls=%async_computation.2 | async-start | bytes 1048576 | tf_op jit(solution)/shard_map/all_to_all | solution.py:144
  90.8 17.4 %all-to-all-start.3 = ((bf16[4,32,2048]{2,1,0:T(8,128)(2,1)}), bf16[4,32,2048]{2,1,0:T(8,128)(2,1)S(1)}, u32[]{:S(2)}, u32[]{:S(2)}) async-start(bf16[4,32,2048]{2,1,0:T(8,128)(2,1)} %broadcast_in_dim.43), calls=%async_computation.3 | async-start | bytes 1048576 | tf_op jit(solution)/shard_map/all_to_all | solution.py:144
  116.8 19.9 %all-to-all-start.4 = ((bf16[4,64,2048]{2,1,0:T(8,128)(2,1)}), bf16[4,64,2048]{2,1,0:T(8,128)(2,1)S(1)}, u32[]{:S(2)}, u32[]{:S(2)}) async-start(bf16[4,64,2048]{2,1,0:T(8,128)(2,1)} %bitcast.121), calls=%async_computation.4 | async-start | bytes 2097152 | tf_op jit(solution)/shard_map/all_to_all | solution.py:218
  136.8 25.9 %all-to-all-start.5 = ((bf16[16,64,256]{2,1,0:T(8,128)(2,1)}), bf16[16,64,256]{2,1,0:T(8,128)(2,1)}, u32[]{:S(2)}, u32[]{:S(2)}) async-start(bf16[16,64,256]{2,1,0:T(8,128)(2,1)} %bitcast.109), calls=%async_computation.5 | async-start | bytes 1048576 | tf_op jit(solution)/shard_map/all_to_all | solution.py:239
  142.4 1.2 copy-start.3
  160.6 2.0 %copy-start.1 = (bf16[8192,256]{1,0:T(8,128)(2,1)}, bf16[8192,256]{1,0:T(8,128)(2,1)S(1)}, u32[]{:S(2)}) copy-start(bf16[8192,256]{1,0:T(8,128)(2,1)S(1)} %shard_map.95.wide_ref) | copy-start | bytes 12582916
  163.7 2.2 %copy-start.2 = (bf16[8192,256]{1,0:T(8,128)(2,1)S(1)}, bf16[8192,256]{1,0:T(8,128)(2,1)}, u32[]{:S(2)}) copy-start(bf16[8192,256]{1,0:T(8,128)(2,1)} %copy-done.1) | copy-start | bytes 12582916
Sparse Core Ops, SparseCore 0:
  9.6 39.6 all-gather.1

commit v3 on v2

--- a/solution.py
+++ b/solution.py
@@ -139,6 +139,32 @@
     )(wide, grad)
 
 
+def mix_kernel(weight_ref, x_ref, out_ref):
+    out_ref[...] = dot(weight_ref[...], x_ref[...]).astype(BF16)
+
+
+def mix(weight, x):
+    outs, rows = weight.shape
+    width = x.shape[1]
+    part = 256
+    return pl.pallas_call(
+        mix_kernel,
+        grid=(width // part,),
+        in_specs=[
+            pl.BlockSpec((outs, rows), lambda i: (0, 0)),
+            pl.BlockSpec((rows, part), lambda i: (0, i)),
+        ],
+        out_specs=pl.BlockSpec((outs, part), lambda i: (0, i)),
+        out_shape=jax.ShapeDtypeStruct((outs, width), BF16),
+        compiler_params=pltpu.CompilerParams(vmem_limit_bytes=32 * 2**20),
+        cost_estimate=pl.CostEstimate(
+            flops=2 * outs * rows * width,
+            bytes_accessed=2 * (outs + width) * rows + 2 * outs * width,
+            transcendentals=0,
+        ),
+    )(weight, x)
+
+
 def gather_all(x, axis):
     shards = lax.axis_size(axis)
     return lax.all_to_all(jnp.broadcast_to(x[None], (shards,) + x.shape), axis, 0, 0, tiled=True)
@@ -170,8 +196,11 @@
     own_b_cols = lax.all_to_all(
         flat_b.reshape(groups, rank_part * SLOTS, kv_part), "dp", 0, 0, tiled=True
     ).reshape(R * SLOTS, kv_part)
+    wide = spread_embed(slot_rows.T, rank_part)
+    slot_rows, own_b_cols, wide = lax.optimization_barrier((slot_rows, own_b_cols, wide))
     every_b = gather_all(own_b_cols, "tensor")
     flat_a = generate(slot_rows, head_a, SLOTS)
+    flat_a, every_b = lax.optimization_barrier((flat_a, every_b))
     own_a = lax.all_to_all(
         flat_a.reshape(groups, rank_part * SLOTS, width), "dp", 0, 0, tiled=True
     ).reshape(R * SLOTS, width)
@@ -193,10 +222,13 @@
     block_weight = 1.0 / (BLOCK * jnp.sum(jnp.where(tenant_hot, count[None, :], 0.0), axis=1))
 
     pick_rows = jnp.repeat(pick, BLOCK, axis=1)
+    partial_t = dot_nt(own_b_cols, target).reshape(R, SLOTS, rows)
+    partial_t = jnp.sum(partial_t * pick_rows[None], axis=1)
+    partial_z = dot_nt(through, tokens).reshape(R, SLOTS, rows)
+    partial_z = jnp.sum(partial_z * pick_rows[None], axis=1) - partial_t
+    own_a, partial_z = lax.optimization_barrier((own_a, partial_z))
     partial_l = dot_nt(own_a, tokens).reshape(R, SLOTS, rows)
-    partial_z = (dot_nt(through, tokens) - dot_nt(own_b_cols, target)).reshape(R, SLOTS, rows)
     partial_l = jnp.sum(partial_l * pick_rows[None], axis=1)
-    partial_z = jnp.sum(partial_z * pick_rows[None], axis=1)
     both = jnp.concatenate([partial_l, partial_z], axis=0).astype(BF16)
     both = jnp.sum(gather_all(both, "tensor").astype(F32), axis=0)
     low_rank = both[:R].astype(BF16)
@@ -212,14 +244,14 @@
     rank_grad = rank_grad.astype(BF16).reshape(R, rows)
 
     pick_bf = pick_rows.astype(BF16)
-    spread_g = (rank_grad[:, None, :] * pick_bf[None]).reshape(R * SLOTS, rows)
+    spread_g = (2.0 * rank_grad[:, None, :] * pick_bf[None]).reshape(R * SLOTS, rows)
     spread_l = (low_rank[:, None, :] * pick_bf[None]).reshape(R * SLOTS, rows)
-    grad_a = (2.0 * dot(spread_g, tokens)).astype(BF16)
+    mixed = mix(jnp.concatenate([spread_g, spread_l], axis=0), tokens)
+    grad_a, low_x = mixed[: R * SLOTS], mixed[R * SLOTS :]
     every_a = lax.all_to_all(
         grad_a.reshape(groups, rank_part * SLOTS, width), "dp", 0, 0, tiled=True
     ).reshape(groups * rank_part * SLOTS, width)
 
-    low_x = dot(spread_l, tokens).astype(BF16)
     gram_l = jnp.einsum("rbm,qbm->brq", low_blocks, low_blocks, preferred_element_type=F32)
     gram_l = jnp.einsum("sb,brq->srq", pick, gram_l, precision=lax.Precision.HIGHEST)
     adapted = jnp.einsum(
@@ -241,7 +273,6 @@
     every_gb = jnp.sum(every_gb, axis=1).astype(BF16)
     every_gb = every_gb.reshape(groups * rank_part * SLOTS, kv_part)
 
-    wide = spread_embed(slot_rows.T, rank_part)
     grad_head_a = head_grad(wide, every_a, rank_part)
     grad_head_b = head_grad(wide, every_gb, rank_part)
     return (grad_head_a, grad_head_b)

time: 179 us -> 164 us (0.916)
  waiting for transfers between devices: 33.4 us -> 20.6 us
  matrix products: 38.2 us -> 25.7 us
  Pallas kernels: 44.4 us -> 51.6 us
  local copies, waits for them, and re-layouts: 16.8 us -> 20.6 us
  other arithmetic: 6.13 us -> 4.28 us
    dot_general x4 -> x3, matrix products: 18.7 us -> 6.32 us  [dot(): return jnp.dot(a, b, preferred_element_type=F32)]
    all_to_all x1, waiting for transfers between devices: 14.5 us -> 2.41 us  [body(): lax.all_to_all(flat_a.reshape(groups, rank_part * SLOTS, width), 'dp', 0,...]
    pallas_call x0 -> x1, Pallas kernels: none -> 7.15 us  [mix(): pl.pallas_call(mix_kernel, grid=(width // part,), in_specs=[pl.BlockSpec(...]
    unnamed x18 -> x20, local copies, waits for them, and re-layouts: 7.98 us -> 13.4 us
    all_to_all x2, waiting for transfers between devices: 18.2 us -> 12.9 us  [gather_all(): lax.all_to_all(jnp.broadcast_to(x[None], (shards,) + x.shape), axis, 0, 0...]
    all_to_all x1, waiting for transfers between devices: 0.01 us -> 4.15 us  [body(): lax.all_to_all(grad_a.reshape(groups, rank_part * SLOTS, width), 'dp', 0,...]
  transfers between devices with their start and end apart: 7 -> 7, of which waited for: 3 -> 4; matrix products, arithmetic and copies ran while one was open for 17% -> 17% of each run, Pallas kernels for 22% -> 24%
where the time goes in v3:
time: 164 us; the launch traced here: 162 us
  Pallas kernels  51.6 us (31%)
  matrix products  25.7 us (16%)
  starting transfers between devices  25.2 us (15%)
  local copies, waits for them, and re-layouts  20.6 us (13%)
  waiting for transfers between devices  20.6 us (13%)
  between operations  14.4 us (9%)
  other arithmetic  4.28 us (3%)
    pallas_call x2, Pallas kernels, generate(): pl.pallas_call(functools.partial(generate_kernel, count), grid=(hidden //...  22.7 us
    pallas_call x2, Pallas kernels, head_grad(): pl.pallas_call(head_grad_kernel, grid=(hidden // STEP,), in_specs=[pl.Blo...  19.1 us
    dot_general x3, matrix products, dot_nt(): lax.dot_general(a, b, (((1,), (1,)), ((), ())), preferred_element_type=F32)  17.9 us
    unnamed x20, local copies, waits for them, and re-layouts  13.4 us
    all_to_all x2, waiting for transfers between devices, gather_all(): lax.all_to_all(jnp.broadcast_to(x[None], (shards,) + x.shape), axis, 0, 0...  12.9 us
    all_to_all x2, starting transfers between devices, gather_all(): lax.all_to_all(jnp.broadcast_to(x[None], (shards,) + x.shape), axis, 0, 0...  10.4 us
    pallas_call x1, Pallas kernels, mix(): pl.pallas_call(mix_kernel, grid=(width // part,), in_specs=[pl.BlockSpec(...  7.15 us
    dot_general x3, matrix products, dot(): return jnp.dot(a, b, preferred_element_type=F32)  6.32 us
  transfers between devices with their start and end apart: 7, of which 4 were waited for; matrix products, arithmetic and copies ran while one was open for 17% of the time, Pallas kernels for 24%

profile of v3, /device:TPU:0, one launch (start us, length us, event | category | flops | bytes accessed | tf_op | source)
XLA Modules:
  0.0 162.4 jit_solution(6319888697757754288)
XLA Ops:
  7.9 0.8 select_reduce_fusion
  8.9 1.1 convolution_convert_fusion.1
  10.2 2.2 %copy-done.5 = bf16[2048,4,256]{2,1,0:T(4,128)(2,1)S(1)} copy-done((bf16[2048,4,256]{2,1,0:T(4,128)(2,1)S(1)}, bf16[2048,4,256]{2,1,0:T(4,128)(2,1)}, u32[]{:S(2)}) %copy-start.5) | copy-done | bytes 4194328
  12.4 4.9 %shard_map.95 = bf16[256,256]{1,0:T(8,128)(2,1)} custom-call(bf16[256,2048]{1,0:T(8,128)(2,1)S(1)} %bitcast.98, bf16[2048,4,256]{2,1,0:T(4,128)(2,1)S(1)} %copy-done.5), custom_call_target="tpu_custom_call" | custom-call | flops 1073741824 | bytes 4194304 | tf_op jit(solution)/shard_map/pallas_call | solution.py:67
  17.3 4.2 %all-to-all-start = ((bf16[4,64,256]{2,1,0:T(8,128)(2,1)}), bf16[4,64,256]{2,1,0:T(8,128)(2,1)S(1)}, u32[]{:S(2)}, u32[]{:S(2)}) async-start(bf16[4,64,256]{2,1,0:T(8,128)(2,1)} %bitcast.3), calls=%async_computation | async-start | bytes 262144 | tf_op jit(solution)/shard_map/all_to_all | solution.py:196
  22.8 2.6 %shard_map.96.wide_ref = bf16[8192,256]{1,0:T(8,128)(2,1)S(1)} custom-call(bf16[2048,256]{1,0:T(8,128)(2,1)S(1)} %copy.20.embed_ref), custom_call_target="tpu_custom_call" | custom-call | flops 1073741824 | bytes 4194304 | tf_op jit(solution)/shard_map/pallas_call | solution.py:99
  25.4 2.0 %copy-done.1 = bf16[8192,256]{1,0:T(8,128)(2,1)} copy-done((bf16[8192,256]{1,0:T(8,128)(2,1)}, bf16[8192,256]{1,0:T(8,128)(2,1)S(1)}, u32[]{:S(2)}) %copy-start.1) | copy-done | bytes 4194328
  28.0 0.8 broadcast_in_dim.34
  28.8 5.4 %all-to-all-start.1 = ((bf16[4,256,256]{1,2,0:T(8,128)(2,1)}), bf16[4,256,256]{1,2,0:T(8,128)(2,1)S(1)}, u32[]{:S(2)}, u32[]{:S(2)}) async-start(bf16[4,256,256]{1,2,0:T(8,128)(2,1)} %broadcast_in_dim.34), calls=%async_computation.1 | async-start | bytes 1048576 | tf_op jit(solution)/shard_map/all_to_all | solution.py:170
  34.2 17.8 %shard_map.97 = bf16[256,2048]{1,0:T(8,128)(2,1)} custom-call(bf16[256,2048]{1,0:T(8,128)(2,1)S(1)} %bitcast.100, bf16[2048,4,2048]{2,1,0:T(4,128)(2,1)} %head_ref.3), custom_call_target="tpu_custom_call" | custom-call | flops 8589934592 | bytes 33554432 | tf_op jit(solution)/shard_map/pallas_call | solution.py:67
  52.0 3.5 %all-to-all-start.2 = ((bf16[4,64,2048]{2,1,0:T(8,128)(2,1)}), bf16[4,64,2048]{2,1,0:T(8,128)(2,1)S(1)}, u32[]{:S(2)}, u32[]{:S(2)}) async-start(bf16[4,64,2048]{2,1,0:T(8,128)(2,1)} %bitcast.6), calls=%async_computation.2 | async-start | bytes 2097152 | tf_op jit(solution)/shard_map/all_to_all | solution.py:204
  55.6 9.4 %fusion.11 = f32[256,2048]{1,0:T(8,128)} fusion(bf16[2048,2048]{1,0:T(8,128)(2,1)} %x_ref.1, bf16[256,1024]{0,1:T(8,128)(2,1)S(1)} %bitcast.111, bf16[2048,1024]{1,0:T(8,128)(2,1)} %all-gather.2.cloned.1.call-done), kind=kOutput, calls=%fused_computation.24 | convolution fusion | flops 3221749760 | bytes 15204352 | tf_op jit(solution)/shard_map/dot_general | solution.py:38
  65.0 2.5 %multiply_reduce_fusion.1 = (f32[16,2048]{1,0:T(8,128)S(1)}, f32[16,2048]{1,0:T(8,128)S(1)}) fusion(f32[16,2048]{1,0:T(8,128)S(1)} %bitcast.113, f32[256,2048]{1,0:T(8,128)} %fusion.11, bf16[256,256]{1,0:T(8,128)(2,1)S(1)} %bitcast.109, bf16[2048,256]{1,0:T(8,128)(2,1)S(1)} %copy-done), kind=kOutput, calls=%fused_computation.4 | convolution fusion | flops 270467072 | bytes 3670016 | tf_op jit(solution)/shard_map/dot_general | solution.py:38
  67.6 2.4 %all-to-all-done.2 = bf16[4,64,2048]{2,1,0:T(8,128)(2,1)S(1)} async-done(((bf16[4,64,2048]{2,1,0:T(8,128)(2,1)}), bf16[4,64,2048]{2,1,0:T(8,128)(2,1)S(1)}, u32[]{:S(2)}, u32[]{:S(2)}) %all-to-all-start.2) | async-done | bytes 1048608 | tf_op jit(solution)/shard_map/all_to_all | solution.py:204
  70.0 6.0 %multiply_reduce_fusion = bf16[16,2048]{1,0:T(8,128)(2,1)S(1)} fusion(f32[16,2048]{1,0:T(8,128)S(1)} %bitcast.114, bf16[256,2048]{1,0:T(8,128)(2,1)S(1)} %bitcast.105, bf16[2048,2048]{1,0:T(8,128)(2,1)} %x_ref.1), kind=kOutput, calls=%fused_computation.3 | convolution fusion | flops 2148499456 | bytes 9633792 | tf_op jit(solution)/shard_map/dot_general | solution.py:38
  76.0 0.8 broadcast_in_dim.40
  76.8 5.0 %all-to-all-start.3 = ((bf16[4,32,2048]{2,1,0:T(8,128)(2,1)}), bf16[4,32,2048]{2,1,0:T(8,128)(2,1)S(1)}, u32[]{:S(2)}, u32[]{:S(2)}) async-start(bf16[4,32,2048]{2,1,0:T(8,128)(2,1)} %broadcast_in_dim.40), calls=%async_computation.3 | async-start | bytes 1048576 | tf_op jit(solution)/shard_map/all_to_all | solution.py:170
  83.2 12.9 %all-to-all-done.3 = bf16[4,32,2048]{2,1,0:T(8,128)(2,1)S(1)} async-done(((bf16[4,32,2048]{2,1,0:T(8,128)(2,1)}), bf16[4,32,2048]{2,1,0:T(8,128)(2,1)S(1)}, u32[]{:S(2)}, u32[]{:S(2)}) %all-to-all-start.3) | async-done | bytes 524320 | tf_op jit(solution)/shard_map/all_to_all | solution.py:170
  97.5 3.4 %copy-done.4 = bf16[2048,2048]{1,0:T(8,128)(2,1)S(1)} copy-done((bf16[2048,2048]{1,0:T(8,128)(2,1)S(1)}, bf16[2048,2048]{1,0:T(8,128)(2,1)}, u32[]{:S(2)}) %copy-start.4) | copy-done | bytes 8388632
  100.9 7.2 %shard_map.98 = bf16[512,2048]{1,0:T(8,128)(2,1)S(1)} custom-call(bf16[512,2048]{1,0:T(8,128)(2,1)S(1)} %pad_maximum_fusion.weight_ref, bf16[2048,2048]{1,0:T(8,128)(2,1)S(1)} %copy-done.4), custom_call_target="tpu_custom_call" | custom-call | flops 4294967296 | bytes 12582912 | tf_op jit(solution)/shard_map/pallas_call | solution.py:150
  108.1 1.3 copy-done.6
  109.4 1.1 slice.19
  110.5 3.5 %all-to-all-start.4 = ((bf16[4,64,2048]{2,1,0:T(8,128)(2,1)}), bf16[4,64,2048]{2,1,0:T(8,128)(2,1)S(1)}, u32[]{:S(2)}, u32[]{:S(2)}) async-start(bf16[4,64,2048]{2,1,0:T(8,128)(2,1)} %bitcast.106), calls=%async_computation.4 | async-start | bytes 2097152 | tf_op jit(solution)/shard_map/all_to_all | solution.py:251
  114.0 4.8 %fusion.7 = f32[256,1024]{1,0:T(8,128)} fusion(bf16[2048,1024]{1,0:T(8,128)(2,1)} %all-gather.2.cloned.1.call-done, bf16[512,2048]{1,0:T(8,128)(2,1)} %copy-done.6), kind=kOutput, calls=%fused_computation.18 | convolution fusion | flops 1073741824 | bytes 6291456 | tf_op jit(solution)/shard_map/dot_general | solution.py:34
  118.8 2.7 %reshape.235 = f32[4,64,4,256]{3,2,1,0:T(4,128)} reshape(f32[256,1024]{1,0:T(8,128)} %fusion.7) | data formatting | bytes 2097152 | tf_op jit(solution)/shard_map/reshape | solution.py:266
  121.9 2.4 %fusion.10 = bf16[4,64,4,256]{3,1,2,0:T(8,128)(2,1)} fusion(f32[4,64,4,256]{3,2,1,0:T(4,128)} %reshape.235, f32[64]{0:T(128)S(1)} %tile.9, f32[4,64,256]{2,1,0:T(8,128)S(1)} %bitcast.117, f32[4]{0:T(128)S(1)} %compare_convert_fusion), kind=kLoop, calls=%fused_computation.22 | loop fusion | flops 1048576 | bytes 1835280 | tf_op jit(solution)/shard_map/convert_element_type | solution.py:268
  124.3 4.1 %all-to-all-done.4 = bf16[4,64,2048]{2,1,0:T(8,128)(2,1)S(1)} async-done(((bf16[4,64,2048]{2,1,0:T(8,128)(2,1)}), bf16[4,64,2048]{2,1,0:T(8,128)(2,1)S(1)}, u32[]{:S(2)}, u32[]{:S(2)}) %all-to-all-start.4) | async-done | bytes 1048608 | tf_op jit(solution)/shard_map/all_to_all | solution.py:251
  128.4 3.6 %all-to-all-start.5 = ((bf16[16,64,256]{2,1,0:T(8,128)(2,1)}), bf16[16,64,256]{2,1,0:T(8,128)(2,1)S(1)}, u32[]{:S(2)}, u32[]{:S(2)}) async-start(bf16[16,64,256]{2,1,0:T(8,128)(2,1)} %bitcast.27), calls=%async_computation.5 | async-start | bytes 1048576 | tf_op jit(solution)/shard_map/all_to_all | solution.py:271
  132.0 2.2 %copy-done.2 = bf16[8192,256]{1,0:T(8,128)(2,1)S(1)} copy-done((bf16[8192,256]{1,0:T(8,128)(2,1)S(1)}, bf16[8192,256]{1,0:T(8,128)(2,1)}, u32[]{:S(2)}) %copy-start.2) | copy-done | bytes 4194328
  134.2 14.5 %shard_map.99 = bf16[2048,4,2048]{2,1,0:T(4,128)(2,1)} custom-call(bf16[8192,256]{1,0:T(8,128)(2,1)S(1)} %copy-done.2, bf16[256,2048]{1,0:T(8,128)(2,1)S(1)} %bitcast.101), custom_call_target="tpu_custom_call" | custom-call | flops 8589934592 | bytes 33554432 | tf_op jit(solution)/shard_map/pallas_call | solution.py:124
  148.7 2.2 %copy-done.3 = bf16[8192,256]{1,0:T(8,128)(2,1)S(1)} copy-done((bf16[8192,256]{1,0:T(8,128)(2,1)S(1)}, bf16[8192,256]{1,0:T(8,128)(2,1)}, u32[]{:S(2)}) %copy-start.3) | copy-done | bytes 4194328
  150.9 4.7 %shard_map.100 = bf16[2048,4,256]{2,1,0:T(4,128)(2,1)} custom-call(bf16[8192,256]{1,0:T(8,128)(2,1)S(1)} %copy-done.3, bf16[256,256]{1,0:T(8,128)(2,1)S(1)} %bitcast.102), custom_call_target="tpu_custom_call" | custom-call | flops 1073741824 | bytes 4194304 | tf_op jit(solution)/shard_map/pallas_call | solution.py:124
  (58 shorter events, 6.2 us)
Async XLA Ops:
  7.2 57.9 %copy-start = (bf16[2048,256]{1,0:T(8,128)(2,1)S(1)}, bf16[2048,256]{1,0:T(8,128)(2,1)}, u32[]{:S(2)}) copy-start(bf16[2048,256]{1,0:T(8,128)(2,1)} %param.9) | copy-start | bytes 3145732
  7.2 14.3 %copy-start.7 = (s32[64]{0:T(128)S(1)}, s32[64]{0:T(128)}, u32[]{:S(2)}) copy-start(s32[64]{0:T(128)} %param.14) | copy-start | bytes 772
  7.2 48.4 %all-gather.2.cloned.1.call-start = ((), (), s32[]{:S(2)}) async-start(), calls=%async_computation.6 | async-start | bytes 5242880 | tf_op jit(solution)/shard_map/all_gather | solution.py:185
  7.9 14.1 %copy-start.8 = (s32[32]{0:T(128)S(1)}, s32[32]{0:T(128)}, u32[]{:S(2)}) copy-start(s32[32]{0:T(128)} %param.15) | copy-start | bytes 388
  10.2 2.2 %copy-start.5 = (bf16[2048,4,256]{2,1,0:T(4,128)(2,1)S(1)}, bf16[2048,4,256]{2,1,0:T(4,128)(2,1)}, u32[]{:S(2)}) copy-start(bf16[2048,4,256]{2,1,0:T(4,128)(2,1)} %head_ref.2) | copy-start | bytes 12582916
  17.3 10.6 %all-to-all-start = ((bf16[4,64,256]{2,1,0:T(8,128)(2,1)}), bf16[4,64,256]{2,1,0:T(8,128)(2,1)S(1)}, u32[]{:S(2)}, u32[]{:S(2)}) async-start(bf16[4,64,256]{2,1,0:T(8,128)(2,1)} %bitcast.3), calls=%async_computation | async-start | bytes 262144 | tf_op jit(solution)/shard_map/all_to_all | solution.py:196
  25.4 2.0 %copy-start.1 = (bf16[8192,256]{1,0:T(8,128)(2,1)}, bf16[8192,256]{1,0:T(8,128)(2,1)S(1)}, u32[]{:S(2)}) copy-start(bf16[8192,256]{1,0:T(8,128)(2,1)S(1)} %shard_map.96.wide_ref) | copy-start | bytes 12582916
  28.8 23.2 %all-to-all-start.1 = ((bf16[4,256,256]{1,2,0:T(8,128)(2,1)}), bf16[4,256,256]{1,2,0:T(8,128)(2,1)S(1)}, u32[]{:S(2)}, u32[]{:S(2)}) async-start(bf16[4,256,256]{1,2,0:T(8,128)(2,1)} %broadcast_in_dim.34), calls=%async_computation.1 | async-start | bytes 1048576 | tf_op jit(solution)/shard_map/all_to_all | solution.py:170
  52.0 18.0 %all-to-all-start.2 = ((bf16[4,64,2048]{2,1,0:T(8,128)(2,1)}), bf16[4,64,2048]{2,1,0:T(8,128)(2,1)S(1)}, u32[]{:S(2)}, u32[]{:S(2)}) async-start(bf16[4,64,2048]{2,1,0:T(8,128)(2,1)} %bitcast.6), calls=%async_computation.2 | async-start | bytes 2097152 | tf_op jit(solution)/shard_map/all_to_all | solution.py:204
  76.8 19.3 %all-to-all-start.3 = ((bf16[4,32,2048]{2,1,0:T(8,128)(2,1)}), bf16[4,32,2048]{2,1,0:T(8,128)(2,1)S(1)}, u32[]{:S(2)}, u32[]{:S(2)}) async-start(bf16[4,32,2048]{2,1,0:T(8,128)(2,1)} %broadcast_in_dim.40), calls=%async_computation.3 | async-start | bytes 1048576 | tf_op jit(solution)/shard_map/all_to_all | solution.py:170
  97.5 3.4 %copy-start.4 = (bf16[2048,2048]{1,0:T(8,128)(2,1)S(1)}, bf16[2048,2048]{1,0:T(8,128)(2,1)}, u32[]{:S(2)}) copy-start(bf16[2048,2048]{1,0:T(8,128)(2,1)} %x_ref.1) | copy-start | bytes 25165828
  108.0 1.3 copy-start.6
  110.5 18.0 %all-to-all-start.4 = ((bf16[4,64,2048]{2,1,0:T(8,128)(2,1)}), bf16[4,64,2048]{2,1,0:T(8,128)(2,1)S(1)}, u32[]{:S(2)}, u32[]{:S(2)}) async-start(bf16[4,64,2048]{2,1,0:T(8,128)(2,1)} %bitcast.106), calls=%async_computation.4 | async-start | bytes 2097152 | tf_op jit(solution)/shard_map/all_to_all | solution.py:251
  128.4 20.2 %all-to-all-start.5 = ((bf16[16,64,256]{2,1,0:T(8,128)(2,1)}), bf16[16,64,256]{2,1,0:T(8,128)(2,1)S(1)}, u32[]{:S(2)}, u32[]{:S(2)}) async-start(bf16[16,64,256]{2,1,0:T(8,128)(2,1)} %bitcast.27), calls=%async_computation.5 | async-start | bytes 1048576 | tf_op jit(solution)/shard_map/all_to_all | solution.py:271
  132.0 2.2 %copy-start.2 = (bf16[8192,256]{1,0:T(8,128)(2,1)S(1)}, bf16[8192,256]{1,0:T(8,128)(2,1)}, u32[]{:S(2)}) copy-start(bf16[8192,256]{1,0:T(8,128)(2,1)} %copy-done.1) | copy-start | bytes 12582916
  148.7 2.2 %copy-start.3 = (bf16[8192,256]{1,0:T(8,128)(2,1)S(1)}, bf16[8192,256]{1,0:T(8,128)(2,1)}, u32[]{:S(2)}) copy-start(bf16[8192,256]{1,0:T(8,128)(2,1)} %copy-done.1) | copy-start | bytes 12582916
Sparse Core Ops, SparseCore 0:
  9.6 39.1 all-gather.1
